TPU v7x, 128 devices: a whole 4x4x4 slice. The times are simulated.
128 devices in a mesh: gx: 8 (over y_lo, x), gy: 16 (over y_hi, z, core).
Axes of the slice: x: 4, y: 4 (y_hi: 2, y_lo: 2; y = y_hi * 2 + y_lo), z: 4, core: 2. Of those that a mesh axis runs over, the one named last changes fastest.
Arguments:
- tokens: bfloat16 [512, 8192], P('gx', 'gy'), may hold values from -12 to 12
- segment_ids: int32 [512], P('gy'), may hold values from 0 to 3, never falling along the last dimension, each value on 1 to 384 neighbouring positions
- attn_gain: bfloat16 [8192], P('gy'), may hold values from 0.5 to 1.5
- query_weight: bfloat16 [8192, 8192], P(('gx', 'gy')), may hold values from -1 to 1
- query_bias: bfloat16 [8192], P('gx'), may hold values from -3 to 3
- key_weight: bfloat16 [1024, 8192], P(('gx', 'gy')), may hold values from -20 to 20
- value_weight: bfloat16 [1024, 8192], P(('gx', 'gy')), may hold values from -0.0625 to 0.0625
- value_bias: bfloat16 [1024], P('gx'), may hold values from -3 to 3
- out_weight: bfloat16 [8192, 8192], P(('gx', 'gy')), may hold values from -0.0625 to 0.0625
- ffn_gain: bfloat16 [8192], P('gy'), may hold values from 0.5 to 1.5
- gate_weight: bfloat16 [29568, 8192], P(('gx', 'gy')), may hold values from -0.0625 to 0.0625
- up_weight: bfloat16 [29568, 8192], P(('gx', 'gy')), may hold values from -0.0625 to 0.0625
- down_weight: bfloat16 [29568, 8192], P(('gx', 'gy')), may hold values from -0.03125 to 0.03125
Outputs:
- mixed: bfloat16 [512, 8192], P('gx', 'gy')
Inputs may be any that keep to these rules, and one draw needn't show every extreme that they name: `segment_ids`: documents occupy consecutive positions, numbers never fall, and one document spans exactly 384 positions.
All inputs are finite; a program needn't handle non-finite values.
Results may differ from a plain program's by a relative error of at most 0.012.
The roundings to bfloat16 on the way count: a program that leaves them out, or rounds other values in their place, can miss the bound.
Values may be sent and summed in bfloat16 or wider, within the bound.
A program may use at most 128 MiB of HBM per device.

v0:
```python
import math

import jax
import jax.numpy as jnp
from jax import lax
from jax.sharding import PartitionSpec as P

HEAD_DIM = 128


EPSILON = 1e-06
ROTARY_BASE = 1000000.0


def project_rows(row_block, weight_rows):
    return lax.dot_general(
        row_block, weight_rows, (((1,), (1,)), ((), ())), preferred_element_type=jnp.float32
    )


def rotate(values, positions):
    row_count = values.shape[0]
    shaped = values.reshape(row_count, -1, HEAD_DIM)
    half_dim = HEAD_DIM // 2
    frequency = jnp.power(
        jnp.float32(ROTARY_BASE), -(jnp.arange(half_dim, dtype=jnp.float32) * 2.0) / HEAD_DIM
    )
    angles = positions[:, None] * frequency[None, :]
    cosine = jnp.cos(angles)[:, None, :]
    sine_part = jnp.sin(angles)[:, None, :]
    first_half = shaped[..., :half_dim]
    second_half = shaped[..., half_dim:]
    turned = jnp.concatenate(
        [
            first_half * cosine - second_half * sine_part,
            second_half * cosine + first_half * sine_part,
        ],
        axis=-1,
    )
    return turned.reshape(row_count, -1)


def normalize(values, feature_gain):
    floats = values.astype(jnp.float32)
    squares = lax.psum(jnp.sum(floats * floats, axis=1), "gy")
    feature_total = values.shape[1] * lax.axis_size("gy")
    inverse = lax.rsqrt(squares / feature_total + EPSILON)
    normed = (floats * inverse[:, None] * feature_gain.astype(jnp.float32)[None, :]).astype(
        jnp.bfloat16
    )
    return lax.all_gather(normed, "gx", axis=0, tiled=True)


def shards(
    tokens,
    segment_ids,
    attn_gain,
    query_weight,
    query_bias,
    key_weight,
    value_weight,
    value_bias,
    out_weight,
    ffn_gain,
    gate_weight,
    up_weight,
    down_weight,
):
    query_block, key_block, value_block, out_block = (
        lax.all_to_all(query_weight, "gy", split_axis=1, concat_axis=0, tiled=True),
        lax.all_to_all(key_weight, "gy", split_axis=1, concat_axis=0, tiled=True),
        lax.all_to_all(value_weight, "gy", split_axis=1, concat_axis=0, tiled=True),
        lax.all_to_all(out_weight, "gy", split_axis=1, concat_axis=0, tiled=True),
    )
    attn_in = normalize(tokens, attn_gain)
    total_rows = attn_in.shape[0]
    local_rows = total_rows // lax.axis_size("gy")
    query_width = query_block.shape[0]
    key_width = key_block.shape[0]
    row_block = attn_in
    qkv_sum = lax.psum_scatter(
        jnp.concatenate(
            [
                project_rows(row_block, query_block),
                project_rows(row_block, key_block),
                project_rows(row_block, value_block),
            ],
            axis=1,
        ),
        "gy",
        scatter_dimension=0,
        tiled=True,
    )
    query_index = lax.axis_index("gy") * local_rows + jnp.arange(local_rows, dtype=jnp.int32)
    positions = query_index.astype(jnp.float32)
    queries = rotate(
        qkv_sum[:, :query_width] + query_bias.astype(jnp.float32)[None, :], positions
    ).astype(jnp.bfloat16)
    keys_own = rotate(qkv_sum[:, query_width : query_width + key_width], positions).astype(
        jnp.bfloat16
    )
    values_own = (
        qkv_sum[:, query_width + key_width :] + value_bias.astype(jnp.float32)[None, :]
    ).astype(jnp.bfloat16)
    keys_all, values_all, segments_all = (
        lax.all_gather(keys_own, "gy", axis=0, tiled=True),
        lax.all_gather(values_own, "gy", axis=0, tiled=True),
        lax.all_gather(segment_ids, "gy", axis=0, tiled=True),
    )
    kv_local = key_width // HEAD_DIM
    group_size = query_width // key_width
    heads_q = queries.reshape(local_rows, kv_local, group_size, HEAD_DIM)
    heads_k = keys_all.reshape(total_rows, kv_local, HEAD_DIM)
    heads_v = values_all.reshape(total_rows, kv_local, HEAD_DIM)
    key_index = jnp.arange(total_rows, dtype=jnp.int32)
    allowed = (key_index[None, :] <= query_index[:, None]) & (
        segments_all[None, :] == segment_ids[:, None]
    )
    scores = jnp.einsum(
        "tkgd,skd->kgts", heads_q, heads_k, preferred_element_type=jnp.float32
    ) / math.sqrt(HEAD_DIM)
    scores = jnp.where(allowed, scores, -jnp.inf)
    row_max = jnp.max(scores, axis=-1, keepdims=True)
    weights = jnp.where(allowed, jnp.exp(scores - row_max), 0.0)
    denominator = jnp.sum(weights, axis=-1)
    probabilities = weights.astype(jnp.bfloat16)
    attended = jnp.einsum(
        "kgts,skd->tkgd", probabilities, heads_v, preferred_element_type=jnp.float32
    )
    attended = attended / denominator.transpose(2, 0, 1)[..., None]
    attended = attended.reshape(local_rows, query_width).astype(jnp.bfloat16)
    attended_all = lax.all_gather(attended, "gy", axis=0, tiled=True)
    row_block = attended_all
    attn_out = lax.psum_scatter(
        jnp.dot(row_block, out_block, preferred_element_type=jnp.float32),
        "gx",
        scatter_dimension=0,
        tiled=True,
    )
    resid = (tokens.astype(jnp.float32) + attn_out).astype(jnp.bfloat16)
    ffn_in = normalize(resid, ffn_gain)
    gate_block, up_block, down_block = (
        lax.all_to_all(gate_weight, "gy", split_axis=1, concat_axis=0, tiled=True),
        lax.all_to_all(up_weight, "gy", split_axis=1, concat_axis=0, tiled=True),
        lax.all_to_all(down_weight, "gy", split_axis=1, concat_axis=0, tiled=True),
    )
    unit_count = gate_block.shape[0]
    row_block = ffn_in
    gate_up = lax.psum_scatter(
        jnp.concatenate(
            [project_rows(row_block, gate_block), project_rows(row_block, up_block)], axis=1
        ),
        "gy",
        scatter_dimension=0,
        tiled=True,
    )
    hidden = (jax.nn.silu(gate_up[:, :unit_count]) * gate_up[:, unit_count:]).astype(jnp.bfloat16)
    hidden_all = lax.all_gather(hidden, "gy", axis=0, tiled=True)
    row_block = hidden_all
    ffn_out = lax.psum_scatter(
        jnp.dot(row_block, down_block, preferred_element_type=jnp.float32),
        "gx",
        scatter_dimension=0,
        tiled=True,
    )
    return (resid.astype(jnp.float32) + ffn_out).astype(jnp.bfloat16)


def solution(mesh):
    placed = (
        P("gx", "gy"),
        P("gy"),
        P("gy"),
        P(("gx", "gy"), None),
        P("gx"),
        P(("gx", "gy"), None),
        P(("gx", "gy"), None),
        P("gx"),
        P(("gx", "gy"), None),
        P("gy"),
        P(("gx", "gy"), None),
        P(("gx", "gy"), None),
        P(("gx", "gy"), None),
    )
    return jax.shard_map(
        shards, mesh=mesh, in_specs=placed, out_specs=P("gx", "gy"), check_vma=False
    )
```

profile of v0, /device:TPU:0, one launch (start us, length us, event | category | flops | bytes accessed | tf_op | source)
XLA Modules:
  0.0 722.9 jit_solution(9981115039944779761)
XLA Ops:
  6.5 16.5 %all_to_all.133 = bf16[8,16,512]{2,0,1:T(8,128)(2,1)S(1)} all-to-all(bf16[8,16,512]{2,0,1:T(8,128)(2,1)} %bitcast.108), channel_id=1, replica_groups=mesh['gx'=8,'gy'=16] {'gy'}, dimensions={1} | all-to-all | bytes 262144 | tf_op jit(solution)/shard_map/all_to_all | solution.py:71
  29.8 38.4 %psum.14 = f32[64]{0:T(128)S(1)} all-reduce(f32[64]{0:T(128)S(1)} %fusion.12), channel_id=1, replica_groups=mesh['gx'=8,'gy'=16] {'gy'}, use_global_device_ids=true, to_apply=%region_1.0 | all-reduce | flops 64 | bytes 512 | tf_op jit(solution)/shard_map/psum | solution.py:45
  72.0 29.4 %all_gather.21 = bf16[512,512]{1,0:T(8,128)(2,1)S(1)} all-gather(bf16[64,512]{1,0:T(8,128)(2,1)S(1)} %fusion.14), channel_id=1, replica_groups=mesh['gx'=8,'gy'=16] {'gx'}, dimensions={0}, use_global_device_ids=true | all-gather | bytes 589824 | tf_op jit(solution)/shard_map/all_gather | solution.py:51
  105.7 7.1 all-to-all-start.3
  121.0 9.7 %all-to-all-done.3 = bf16[64,16,512]{2,0,1:T(8,128)(2,1)S(1)} async-done(((bf16[64,16,512]{2,0,1:T(8,128)(2,1)}), bf16[64,16,512]{2,0,1:T(8,128)(2,1)S(1)}, u32[]{:S(2)}, u32[]{:S(2)}) %all-to-all-start.3) | async-done | bytes 1048608 | tf_op jit(solution)/shard_map/all_to_all | solution.py:73
  130.8 4.5 all-to-all-start.4
  137.0 56.4 %all-reduce = s32[512]{0:T(512)S(1)} all-reduce(s32[512]{0:T(512)S(1)} %dynamic-update-slice), channel_id=1, replica_groups=mesh['gx'=8,'gy'=16] {'gy'}, use_global_device_ids=true, to_apply=%add | all-reduce | flops 512 | bytes 4096
  193.6 14.2 %reduce-scatter.7.cloned.1.call-done = f32[32,1280]{1,0:T(8,128)} async-done(((f32[512,1280]{1,0:T(8,128)}), f32[32,1280]{1,0:T(8,128)}) %reduce-scatter.7.cloned.1.call-update) | async-done | bytes 163856 | tf_op jit(solution)/shard_map/reduce_scatter | solution.py:81
  209.7 21.8 %all-gather = bf16[512,1,128]{2,0,1:T(8,128)(2,1)S(1)} all-gather(bf16[32,1,128]{2,0,1:T(8,128)(2,1)S(1)} %pad_maximum_fusion.2), channel_id=2, replica_groups=mesh['gx'=8,'gy'=16] {'gy'}, dimensions={0}, use_global_device_ids=true | all-gather | bytes 139264 | tf_op jit(solution)/shard_map/all_gather | solution.py:106
  231.5 19.8 %all_gather.22 = bf16[512,128]{1,0:T(8,128)(2,1)S(1)} all-gather(bf16[32,128]{1,0:T(8,128)(2,1)S(1)} %get-tuple-element.9), channel_id=1, replica_groups=mesh['gx'=8,'gy'=16] {'gy'}, dimensions={0}, use_global_device_ids=true | all-gather | bytes 139264 | tf_op jit(solution)/shard_map/all_gather | solution.py:107
  257.1 4.1 copy.55
  261.3 5.5 all-to-all-start.5
  266.9 59.0 %all-gather.4.cloned.1.call-done = bf16[512,1024]{1,0:T(8,128)(2,1)} async-done(((bf16[32,1024]{1,0:T(8,128)(2,1)}), bf16[512,1024]{1,0:T(8,128)(2,1)}) %all-gather.4.cloned.1.call-update) | async-done | bytes 1048592 | tf_op jit(solution)/shard_map/all_gather | solution.py:132
  336.8 35.6 %reduce-scatter.9.cloned.1.call-done = f32[64,512]{1,0:T(8,128)} async-done(((f32[512,512]{1,0:T(8,128)}), f32[64,512]{1,0:T(8,128)}) %reduce-scatter.9.cloned.1.call-update) | async-done | bytes 131088 | tf_op jit(solution)/shard_map/reduce_scatter | solution.py:134
  373.4 33.2 %psum.15 = f32[64]{0:T(128)S(1)} all-reduce(f32[64]{0:T(128)S(1)} %get-tuple-element.5), channel_id=1, replica_groups=mesh['gx'=8,'gy'=16] {'gy'}, use_global_device_ids=true, to_apply=%region_7.8 | all-reduce | flops 64 | bytes 512 | tf_op jit(solution)/shard_map/psum | solution.py:45
  406.7 29.1 %all_gather.26 = bf16[512,512]{1,0:T(8,128)(2,1)S(1)} all-gather(bf16[64,512]{1,0:T(8,128)(2,1)S(1)} %fusion.18), channel_id=1, replica_groups=mesh['gx'=8,'gy'=16] {'gx'}, dimensions={0}, use_global_device_ids=true | all-gather | bytes 589824 | tf_op jit(solution)/shard_map/all_gather | solution.py:51
  435.8 4.4 fusion.48
  442.5 6.2 pad_maximum_fusion
  448.7 15.3 %copy.61 = f32[512,7392]{1,0:T(8,128)} copy(f32[512,7392]{0,1:T(8,128)} %pad_maximum_fusion) | data formatting | bytes 30277632
  464.1 131.9 %reduce-scatter.13.cloned.1.call-done = f32[32,7392]{1,0:T(8,128)} async-done(((f32[512,7392]{1,0:T(8,128)}), f32[32,7392]{1,0:T(8,128)}) %reduce-scatter.13.cloned.1.call-update) | async-done | bytes 946192 | tf_op jit(solution)/shard_map/reduce_scatter | solution.py:149
  604.4 62.1 %all_to_all.134 = bf16[231,16,512]{2,0,1:T(8,128)(2,1)} all-to-all(bf16[231,16,512]{2,0,1:T(8,128)(2,1)S(1)} %copy.58), channel_id=1, replica_groups=mesh['gx'=8,'gy'=16] {'gy'}, dimensions={1} | all-to-all | bytes 7569408 | tf_op jit(solution)/shard_map/all_to_all | solution.py:145
  666.4 4.1 all_to_all.125
  671.2 6.4 fusion.50
  677.6 36.9 %reduce-scatter.11.cloned.1.call-done = f32[64,512]{1,0:T(8,128)} async-done(((f32[512,512]{1,0:T(8,128)}), f32[64,512]{1,0:T(8,128)}) %reduce-scatter.11.cloned.1.call-update) | async-done | bytes 131088 | tf_op jit(solution)/shard_map/reduce_scatter | solution.py:160
  (87 shorter events, 57.0 us)
Async XLA Ops:
  6.5 65.4 %copy-start.2 = (bf16[64,512]{1,0:T(8,128)(2,1)S(1)}, bf16[64,512]{1,0:T(8,128)(2,1)}, u32[]{:S(2)}) copy-start(bf16[64,512]{1,0:T(8,128)(2,1)} %param.13) | copy-start | bytes 196612
  6.5 65.4 %copy-start.4 = (bf16[512]{0:T(512)(128)(2,1)S(1)}, bf16[512]{0:T(512)(128)(2,1)}, u32[]{:S(2)}) copy-start(bf16[512]{0:T(512)(128)(2,1)} %param.15) | copy-start | bytes 3076
  23.0 45.2 %all-to-all-start.2 = ((bf16[8,16,512]{2,0,1:T(8,128)(2,1)}), bf16[8,16,512]{2,0,1:T(8,128)(2,1)S(1)}, u32[]{:S(2)}, u32[]{:S(2)}) async-start(bf16[8,16,512]{2,0,1:T(8,128)(2,1)} %bitcast.109), calls=%async_computation.2 | async-start | bytes 262144 | tf_op jit(solution)/shard_map/all_to_all | solution.py:72
  68.2 33.8 %all-to-all-start = ((bf16[64,16,512]{2,0,1:T(8,128)(2,1)}), bf16[64,16,512]{2,0,1:T(8,128)(2,1)S(1)}, u32[]{:S(2)}, u32[]{:S(2)}) async-start(bf16[64,16,512]{2,0,1:T(8,128)(2,1)} %bitcast.92), calls=%async_computation | async-start | bytes 2097152 | tf_op jit(solution)/shard_map/all_to_all | solution.py:70
  71.9 135.9 %reduce-scatter.7.cloned.1.call-start = ((), (), s32[]{:S(2)}) async-start(), calls=%async_computation.11 | async-start | bytes 2785280 | tf_op jit(solution)/shard_map/reduce_scatter | solution.py:81
  102.8 1.8 copy-start.1
  105.7 25.1 %all-to-all-start.3 = ((bf16[64,16,512]{2,0,1:T(8,128)(2,1)}), bf16[64,16,512]{2,0,1:T(8,128)(2,1)S(1)}, u32[]{:S(2)}, u32[]{:S(2)}) async-start(bf16[64,16,512]{2,0,1:T(8,128)(2,1)} %bitcast.91), calls=%async_computation.4 | async-start | bytes 2097152 | tf_op jit(solution)/shard_map/all_to_all | solution.py:73
  121.0 14.4 %copy-start.7 = (bf16[128]{0:T(256)(128)(2,1)S(1)}, bf16[128]{0:T(256)(128)(2,1)}, u32[]{:S(2)}) copy-start(bf16[128]{0:T(256)(128)(2,1)} %param.20) | copy-start | bytes 772
  121.0 14.4 %copy-start.3 = (bf16[1024]{0:T(1024)(128)(2,1)S(1)}, bf16[1024]{0:T(1024)(128)(2,1)}, u32[]{:S(2)}) copy-start(bf16[1024]{0:T(1024)(128)(2,1)} %param.17) | copy-start | bytes 6148
  121.0 14.4 %copy-start.8 = (u32[128]{0:T(128)S(1)}, u32[128]{0:T(128)}, u32[]{:S(2)}) copy-start(u32[128]{0:T(128)} %constant.38) | copy-start | bytes 1540
  121.0 15.7 %copy-start.6 = (s32[32]{0:T(128)S(1)}, s32[32]{0:T(128)}, u32[]{:S(2)}) copy-start(s32[32]{0:T(128)} %param.14) | copy-start | bytes 388
  130.8 130.5 %all-to-all-start.4 = ((bf16[231,16,512]{2,0,1:T(8,128)(2,1)}), bf16[231,16,512]{2,0,1:T(8,128)(2,1)}, u32[]{:S(2)}, u32[]{:S(2)}) async-start(bf16[231,16,512]{2,0,1:T(8,128)(2,1)} %copy.54), calls=%async_computation.6 | async-start | bytes 7602176 | tf_op jit(solution)/shard_map/all_to_all | solution.py:143
  135.3 190.5 %all-gather.4.cloned.1.call-start = ((), (), s32[]{:S(2)}) async-start(), calls=%async_computation.12 | async-start | bytes 1114112 | tf_op jit(solution)/shard_map/all_gather | solution.py:132
  261.3 71.6 %all-to-all-start.5 = ((bf16[231,16,512]{2,0,1:T(8,128)(2,1)}), bf16[231,16,512]{2,0,1:T(8,128)(2,1)}, u32[]{:S(2)}, u32[]{:S(2)}) async-start(bf16[231,16,512]{2,0,1:T(8,128)(2,1)} %copy.55), calls=%async_computation.7 | async-start | bytes 7602176 | tf_op jit(solution)/shard_map/all_to_all | solution.py:144
  266.8 62.1 %copy-start.5 = (bf16[512]{0:T(512)(128)(2,1)S(1)}, bf16[512]{0:T(512)(128)(2,1)}, u32[]{:S(2)}) copy-start(bf16[512]{0:T(512)(128)(2,1)} %param.22) | copy-start | bytes 3076
  266.8 105.6 %reduce-scatter.9.cloned.1.call-start = ((), (), s32[]{:S(2)}) async-start(), calls=%async_computation.13 | async-start | bytes 1179648 | tf_op jit(solution)/shard_map/reduce_scatter | solution.py:134
  328.8 267.2 %reduce-scatter.13.cloned.1.call-start = ((), (), s32[]{:S(2)}) async-start(), calls=%async_computation.16 | async-start | bytes 16154624 | tf_op jit(solution)/shard_map/reduce_scatter | solution.py:149
  435.8 4.4 copy-start
  464.1 207.1 %all-gather.6.cloned.1.call-start = ((), (), s32[]{:S(2)}) async-start(), calls=%async_computation.14 | async-start | bytes 4038656 | tf_op jit(solution)/shard_map/all_gather | solution.py:158
  598.1 116.4 %reduce-scatter.11.cloned.1.call-start = ((), (), s32[]{:S(2)}) async-start(), calls=%async_computation.15 | async-start | bytes 1179648 | tf_op jit(solution)/shard_map/reduce_scatter | solution.py:160
Sparse Core Ops, SparseCore 0:
  104.7 103.0 reduce-scatter.6
  253.1 72.6 all-gather.3
  328.9 43.4 reduce-scatter.8
  464.2 131.7 reduce-scatter.12
  598.6 72.5 all-gather.5
  677.8 36.6 reduce-scatter.10
where the time goes:
time: 724 us; the launch traced here: 723 us
  blocking collectives  307 us (42%)
  waiting for transfers between devices  288 us (40%)
  local copies, waits for them, and re-layouts  55.1 us (8%)
  starting transfers between devices  24.6 us (3%)
  matrix products  18 us (2%)
  other arithmetic  16.2 us (2%)
  between operations  14.5 us (2%)
    reduce_scatter x1, waiting for transfers between devices, shards(): lax.psum_scatter(jnp.concatenate([project_rows(row_block, gate_block), pr...  132 us
    psum x2, blocking collectives, normalize(): squares = lax.psum(jnp.sum(floats * floats, axis=1), 'gy')  71.6 us
    all_to_all x1, blocking collectives, shards(): lax.all_to_all(down_weight, 'gy', split_axis=1, concat_axis=0, tiled=True)  62.1 us
    all_gather x1, waiting for transfers between devices, shards(): attended_all = lax.all_gather(attended, 'gy', axis=0, tiled=True)  59 us
    all_gather x2, blocking collectives, normalize(): return lax.all_gather(normed, 'gx', axis=0, tiled=True)  58.5 us
    unnamed x1, blocking collectives  56.4 us
    reduce_scatter x1, waiting for transfers between devices, shards(): lax.psum_scatter(jnp.dot(row_block, down_block, preferred_element_type=jn...  36.9 us
    reduce_scatter x1, waiting for transfers between devices, shards(): lax.psum_scatter(jnp.dot(row_block, out_block, preferred_element_type=jnp...  35.6 us
  transfers between devices with their start and end apart: 11, of which 7 were waited for; matrix products, arithmetic and copies ran while one was open for 5% of the time, Pallas kernels for 0%

commit v1 on v0

v1 whole, which is shorter than its diff:
```python
import math

import jax
import jax.numpy as jnp
from jax import lax
from jax.sharding import PartitionSpec as P

HEAD_DIM = 128


EPSILON = 1e-06
ROTARY_BASE = 1000000.0


def project_rows(row_block, weight_rows):
    return lax.dot_general(
        row_block, weight_rows, (((1,), (1,)), ((), ())), preferred_element_type=jnp.float32
    )


def rotate(values, positions):
    row_count = values.shape[0]
    shaped = values.reshape(row_count, -1, HEAD_DIM)
    half_dim = HEAD_DIM // 2
    frequency = jnp.power(
        jnp.float32(ROTARY_BASE), -(jnp.arange(half_dim, dtype=jnp.float32) * 2.0) / HEAD_DIM
    )
    angles = positions[:, None] * frequency[None, :]
    cosine = jnp.cos(angles)[:, None, :]
    sine_part = jnp.sin(angles)[:, None, :]
    first_half = shaped[..., :half_dim]
    second_half = shaped[..., half_dim:]
    turned = jnp.concatenate(
        [
            first_half * cosine - second_half * sine_part,
            second_half * cosine + first_half * sine_part,
        ],
        axis=-1,
    )
    return turned.reshape(row_count, -1)


def normalize(values, feature_gain):
    floats = values.astype(jnp.float32)
    squares = lax.psum(jnp.sum(floats * floats, axis=1), "gy")
    feature_total = values.shape[1] * lax.axis_size("gy")
    inverse = lax.rsqrt(squares / feature_total + EPSILON)
    normed = (floats * inverse[:, None] * feature_gain.astype(jnp.float32)[None, :]).astype(
        jnp.bfloat16
    )
    by_row = lax.all_gather(normed, "gx", axis=0, tiled=True)
    return lax.all_gather(by_row, "gy", axis=1, tiled=True)


def scatter_sum(partial):
    by_row = lax.psum_scatter(
        partial.astype(jnp.bfloat16), "gx", scatter_dimension=0, tiled=True
    )
    return lax.psum_scatter(by_row, "gy", scatter_dimension=1, tiled=True).astype(jnp.float32)


def shards(
    tokens,
    segment_ids,
    attn_gain,
    query_weight,
    query_bias,
    key_weight,
    value_weight,
    value_bias,
    out_weight,
    ffn_gain,
    gate_weight,
    up_weight,
    down_weight,
):
    attn_in = normalize(tokens, attn_gain)
    total_rows = attn_in.shape[0]
    local_rows = total_rows // lax.axis_size("gy")
    query_sum = project_rows(attn_in, query_weight)
    keys_own = project_rows(attn_in, key_weight)
    values_own = project_rows(attn_in, value_weight)
    query_sum = lax.all_to_all(query_sum, "gy", split_axis=0, concat_axis=1, tiled=True)
    kv_all = lax.all_gather(
        jnp.stack([keys_own, values_own], axis=0), "gy", axis=2, tiled=True
    )
    query_width = query_sum.shape[1]
    query_index = lax.axis_index("gy") * local_rows + jnp.arange(local_rows, dtype=jnp.int32)
    positions = query_index.astype(jnp.float32)
    queries = rotate(query_sum + query_bias.astype(jnp.float32)[None, :], positions).astype(
        jnp.bfloat16
    )
    key_index = jnp.arange(total_rows, dtype=jnp.int32)
    keys_all = rotate(kv_all[0], key_index.astype(jnp.float32)).astype(jnp.bfloat16)
    values_all = (kv_all[1] + value_bias.astype(jnp.float32)[None, :]).astype(jnp.bfloat16)
    segments_all = lax.all_gather(segment_ids, "gy", axis=0, tiled=True)
    heads_q = queries.reshape(local_rows, -1, HEAD_DIM)
    allowed = (key_index[None, :] <= query_index[:, None]) & (
        segments_all[None, :] == segment_ids[:, None]
    )
    scores = jnp.einsum(
        "tgd,sd->gts", heads_q, keys_all, preferred_element_type=jnp.float32
    ) / math.sqrt(HEAD_DIM)
    scores = jnp.where(allowed, scores, -jnp.inf)
    row_max = jnp.max(scores, axis=-1, keepdims=True)
    weights = jnp.where(allowed, jnp.exp(scores - row_max), 0.0)
    denominator = jnp.sum(weights, axis=-1)
    probabilities = weights.astype(jnp.bfloat16)
    attended = jnp.einsum("gts,sd->tgd", probabilities, values_all, preferred_element_type=jnp.float32)
    attended = attended / denominator.transpose(1, 0)[..., None]
    attended = attended.reshape(local_rows, query_width).astype(jnp.bfloat16)
    attended = lax.all_to_all(attended, "gy", split_axis=1, concat_axis=0, tiled=True)
    attn_out = scatter_sum(jnp.dot(attended, out_weight, preferred_element_type=jnp.float32))
    resid = (tokens.astype(jnp.float32) + attn_out).astype(jnp.bfloat16)
    ffn_in = normalize(resid, ffn_gain)
    gate = project_rows(ffn_in, gate_weight)
    up = project_rows(ffn_in, up_weight)
    hidden = (jax.nn.silu(gate) * up).astype(jnp.bfloat16)
    ffn_out = scatter_sum(jnp.dot(hidden, down_weight, preferred_element_type=jnp.float32))
    return (resid.astype(jnp.float32) + ffn_out).astype(jnp.bfloat16)


def solution(mesh):
    placed = (
        P("gx", "gy"),
        P("gy"),
        P("gy"),
        P(("gx", "gy"), None),
        P("gx"),
        P(("gx", "gy"), None),
        P(("gx", "gy"), None),
        P("gx"),
        P(("gx", "gy"), None),
        P("gy"),
        P(("gx", "gy"), None),
        P(("gx", "gy"), None),
        P(("gx", "gy"), None),
    )
    return jax.shard_map(
        shards, mesh=mesh, in_specs=placed, out_specs=P("gx", "gy"), check_vma=False
    )
```

time: 724 us -> 708 us (0.978)
  waiting for transfers between devices: 288 us -> 455 us
  blocking collectives: 307 us -> 180 us
  local copies, waits for them, and re-layouts: 55.1 us -> 4.29 us
  matrix products: 18 us -> 40.9 us
  starting transfers between devices: 24.6 us -> 3.72 us
    reduce_scatter x4, waiting for transfers between devices: 218 us -> 319 us  [the longest x2 180 us: scatter_sum(): lax.psum_scatter(partial.astype(jnp.bfloat16), 'gx', scatter_dimension=0,...]
    all_gather x2, waiting for transfers between devices: 59.7 us -> 135 us  [normalize(): return lax.all_gather(by_row, 'gy', axis=1, tiled=True)]
    all_to_all x2 -> x1, blocking collectives: 78.5 us -> 10.2 us  [shards(): lax.all_to_all(attended, 'gy', split_axis=1, concat_axis=0, tiled=True)]
    unnamed x1, blocking collectives: 56.4 us -> 8.91 us
    all_to_all x11 -> x3, local copies, waits for them, and re-layouts: 26.8 us -> 0.77 us  [shards(): lax.all_to_all(query_sum, 'gy', split_axis=0, concat_axis=1, tiled=True)]
    unnamed x27 -> x21, local copies, waits for them, and re-layouts: 28.1 us -> 3.34 us
    all_to_all x5 -> x1, starting transfers between devices: 24.3 us -> 3.51 us  [shards(): lax.all_to_all(query_sum, 'gy', split_axis=0, concat_axis=1, tiled=True)]
    dot_general x5 -> x4, matrix products: 8.04 us -> 20.8 us  [project_rows(): lax.dot_general(row_block, weight_rows, (((1,), (1,)), ((), ())), preferr...]
  transfers between devices with their start and end apart: 11 -> 7, of which waited for: 7 -> 6; matrix products, arithmetic and copies ran while one was open for 5% -> 2% of each run, Pallas kernels for 0% -> 0%
where the time goes in v1:
time: 708 us
  waiting for transfers between devices  455 us (64%)
  blocking collectives  180 us (25%)
  matrix products  40.9 us (6%)
  between operations  14.4 us (2%)
  other arithmetic  9.96 us (1%)
    reduce_scatter x2, waiting for transfers between devices, scatter_sum(): lax.psum_scatter(partial.astype(jnp.bfloat16), 'gx', scatter_dimension=0,...  180 us
    reduce_scatter x2, waiting for transfers between devices, scatter_sum(): lax.psum_scatter(by_row, 'gy', scatter_dimension=1, tiled=True)  139 us
    all_gather x2, waiting for transfers between devices, normalize(): return lax.all_gather(by_row, 'gy', axis=1, tiled=True)  135 us
    psum x2, blocking collectives, normalize(): squares = lax.psum(jnp.sum(floats * floats, axis=1), 'gy')  72.7 us
    all_gather x2, blocking collectives, normalize(): by_row = lax.all_gather(normed, 'gx', axis=0, tiled=True)  62 us
    all_gather x1, blocking collectives, shards(): lax.all_gather(jnp.stack([keys_own, values_own], axis=0), 'gy', axis=2, t...  25.9 us
    dot_general x4, matrix products, project_rows(): lax.dot_general(row_block, weight_rows, (((1,), (1,)), ((), ())), preferr...  20.8 us
  transfers between devices with their start and end apart: 7, of which 6 were waited for; matrix products, arithmetic and copies ran while one was open for 2% of the time, Pallas kernels for 0%

profile of v1, /device:TPU:0, one launch (start us, length us, event | category | flops | bytes accessed | tf_op | source)
XLA Modules:
  0.0 707.8 jit_solution(4633184952033415246)
XLA Ops:
  6.5 1.1 fusion.24
  7.6 39.3 %psum.14 = f32[64]{0:T(128)S(1)} all-reduce(f32[64]{0:T(128)S(1)} %fusion.24), channel_id=1, replica_groups=mesh['gx'=8,'gy'=16] {'gy'}, use_global_device_ids=true, to_apply=%region_1.0 | all-reduce | flops 64 | bytes 512 | tf_op jit(solution)/shard_map/psum | solution.py:45
  48.6 30.9 %all_gather.18 = bf16[512,512]{1,0:T(8,128)(2,1)} all-gather(bf16[64,512]{1,0:T(8,128)(2,1)S(1)} %fusion.26), channel_id=1, replica_groups=mesh['gx'=8,'gy'=16] {'gx'}, dimensions={0}, use_global_device_ids=true | all-gather | bytes 589824 | tf_op jit(solution)/shard_map/all_gather | solution.py:51
  80.1 1.2 dynamic-slice
  82.9 8.9 %all-reduce = s32[512]{0:T(512)S(1)} all-reduce(s32[512]{0:T(512)S(1)} %dynamic-update-slice), channel_id=1, replica_groups=mesh['gx'=8,'gy'=16] {'gy'}, use_global_device_ids=true, to_apply=%add | all-reduce | flops 512 | bytes 4096
  93.4 60.1 %all-gather.3.cloned.1.call-done = bf16[512,8192]{1,0:T(8,128)(2,1)} async-done(((bf16[512,512]{1,0:T(8,128)(2,1)}), bf16[512,8192]{1,0:T(8,128)(2,1)}) %all-gather.3.cloned.1.call-update) | async-done | bytes 8388624 | tf_op jit(solution)/shard_map/all_gather | solution.py:52
  153.6 5.9 fusion.68
  160.3 3.5 all-to-all-start
  163.9 5.8 convolution_bitcast_fusion.1
  169.7 2.3 convolution_bitcast_fusion.2
  172.0 25.9 %all_gather.20 = f32[2,512,128]{1,2,0:T(8,128)S(1)} all-gather(f32[2,512,8]{1,2,0:T(8,128)S(1)} %pad_maximum_fusion), channel_id=1, replica_groups=mesh['gx'=8,'gy'=16] {'gy'}, dimensions={2}, use_global_device_ids=true | all-gather | bytes 557056 | tf_op jit(solution)/shard_map/all_gather | solution.py:84
  201.7 10.2 %all_to_all.35 = bf16[16,2,1024]{2,1,0:T(2,128)(2,1)S(1)} all-to-all(bf16[16,2,1024]{2,1,0:T(2,128)(2,1)S(1)} %reshape.187), channel_id=1, replica_groups=mesh['gx'=8,'gy'=16] {'gy'}, dimensions={0} | all-to-all | bytes 131072 | tf_op jit(solution)/shard_map/all_to_all | solution.py:112
  212.2 5.5 convolution_convert_fusion.1
  217.8 89.7 %reduce-scatter.5.cloned.1.call-done = bf16[64,8192]{1,0:T(8,128)(2,1)} async-done(((bf16[512,8192]{1,0:T(8,128)(2,1)}), bf16[64,8192]{1,0:T(8,128)(2,1)}) %reduce-scatter.5.cloned.1.call-update) | async-done | bytes 1048592 | tf_op jit(solution)/shard_map/reduce_scatter | solution.py:56
  307.6 69.5 %reduce-scatter.7.cloned.1.call-done = bf16[64,512]{1,0:T(8,128)(2,1)} async-done(((bf16[64,8192]{1,0:T(8,128)(2,1)}), bf16[64,512]{1,0:T(8,128)(2,1)}) %reduce-scatter.7.cloned.1.call-update) | async-done | bytes 65552 | tf_op jit(solution)/shard_map/reduce_scatter | solution.py:59
  377.1 1.0 fusion.28
  378.1 33.4 %psum.15 = f32[64]{0:T(128)S(1)} all-reduce(f32[64]{0:T(128)S(1)} %fusion.28), channel_id=1, replica_groups=mesh['gx'=8,'gy'=16] {'gy'}, use_global_device_ids=true, to_apply=%region_7.8 | all-reduce | flops 64 | bytes 512 | tf_op jit(solution)/shard_map/psum | solution.py:45
  412.4 31.2 %all_gather.22 = bf16[512,512]{1,0:T(8,128)(2,1)} all-gather(bf16[64,512]{1,0:T(8,128)(2,1)S(1)} %fusion.30), channel_id=1, replica_groups=mesh['gx'=8,'gy'=16] {'gx'}, dimensions={0}, use_global_device_ids=true | all-gather | bytes 589824 | tf_op jit(solution)/shard_map/all_gather | solution.py:51
  443.6 75.2 %all-gather.5.cloned.1.call-done = bf16[512,8192]{1,0:T(8,128)(2,1)} async-done(((bf16[512,512]{1,0:T(8,128)(2,1)}), bf16[512,8192]{1,0:T(8,128)(2,1)}) %all-gather.5.cloned.1.call-update) | async-done | bytes 8388624 | tf_op jit(solution)/shard_map/all_gather | solution.py:52
  518.8 6.8 fusion.69
  525.7 13.6 %convolution_convert_fusion = bf16[512,8192]{1,0:T(8,128)(2,1)} fusion(bf16[231,8192]{1,0:T(8,128)(2,1)} %param.25, bf16[512,8192]{1,0:T(8,128)(2,1)} %all-gather.5.cloned.1.call-done, bf16[231,8192]{1,0:T(8,128)(2,1)} %param.24, f32[512,231]{0,1:T(8,128)S(1)} %fusion.69), kind=kOutput, calls=%fused_computation.1 | convolution fusion | flops 3880440832 | bytes 24819712 | tf_op jit(solution)/shard_map/dot_general | solution.py:119
  539.4 90.2 %reduce-scatter.9.cloned.1.call-done = bf16[64,8192]{1,0:T(8,128)(2,1)} async-done(((bf16[512,8192]{1,0:T(8,128)(2,1)}), bf16[64,8192]{1,0:T(8,128)(2,1)}) %reduce-scatter.9.cloned.1.call-update) | async-done | bytes 1048592 | tf_op jit(solution)/shard_map/reduce_scatter | solution.py:56
  629.5 69.9 %reduce-scatter.11.cloned.1.call-done = bf16[64,512]{1,0:T(8,128)(2,1)} async-done(((bf16[64,8192]{1,0:T(8,128)(2,1)}), bf16[64,512]{1,0:T(8,128)(2,1)}) %reduce-scatter.11.cloned.1.call-update) | async-done | bytes 65552 | tf_op jit(solution)/shard_map/reduce_scatter | solution.py:59
  699.5 1.5 fusion.31
  (61 shorter events, 10.8 us)
Async XLA Ops:
  6.5 205.6 %copy-start = (bf16[64,8192]{1,0:T(8,128)(2,1)S(1)}, bf16[64,8192]{1,0:T(8,128)(2,1)}, u32[]{:S(2)}) copy-start(bf16[64,8192]{1,0:T(8,128)(2,1)} %param.21) | copy-start | bytes 3145732
  6.5 157.4 %copy-start.4 = (bf16[8,8192]{1,0:T(8,128)(2,1)S(1)}, bf16[8,8192]{1,0:T(8,128)(2,1)}, u32[]{:S(2)}) copy-start(bf16[8,8192]{1,0:T(8,128)(2,1)} %param.19) | copy-start | bytes 393220
  6.5 147.0 %all-gather.3.cloned.1.call-start = ((), (), s32[]{:S(2)}) async-start(), calls=%async_computation.6 | async-start | bytes 8912896 | tf_op jit(solution)/shard_map/all_gather | solution.py:52
  93.4 76.3 %copy-start.5 = (bf16[8,8192]{1,0:T(8,128)(2,1)S(1)}, bf16[8,8192]{1,0:T(8,128)(2,1)}, u32[]{:S(2)}) copy-start(bf16[8,8192]{1,0:T(8,128)(2,1)} %param.18) | copy-start | bytes 393220
  160.3 38.1 %all-to-all-start = ((f32[16,1,2048]{2,1,0:T(1,128)}), f32[16,1,2048]{2,1,0:T(1,128)S(1)}, u32[]{:S(2)}, u32[]{:S(2)}) async-start(f32[16,1,2048]{2,1,0:T(1,128)} %reshape.185), calls=%async_computation | async-start | bytes 262144 | tf_op jit(solution)/shard_map/all_to_all | solution.py:83
  163.8 143.6 %reduce-scatter.5.cloned.1.call-start = ((), (), s32[]{:S(2)}) async-start(), calls=%async_computation.7 | async-start | bytes 9437184 | tf_op jit(solution)/shard_map/reduce_scatter | solution.py:56
  163.9 5.8 copy-start.1
  212.1 95.4 %copy-start.6 = (bf16[512]{0:T(512)(128)(2,1)S(1)}, bf16[512]{0:T(512)(128)(2,1)}, u32[]{:S(2)}) copy-start(bf16[512]{0:T(512)(128)(2,1)} %param.22) | copy-start | bytes 3076
  212.2 165.0 %copy-start.2 = (bf16[64,512]{1,0:T(8,128)(2,1)S(1)}, bf16[64,512]{1,0:T(8,128)(2,1)}, u32[]{:S(2)}) copy-start(bf16[64,512]{1,0:T(8,128)(2,1)} %param.13) | copy-start | bytes 196612
  217.7 159.4 %reduce-scatter.7.cloned.1.call-start = ((), (), s32[]{:S(2)}) async-start(), calls=%async_computation.8 | async-start | bytes 1114112 | tf_op jit(solution)/shard_map/reduce_scatter | solution.py:59
  307.5 211.3 %all-gather.5.cloned.1.call-start = ((), (), s32[]{:S(2)}) async-start(), calls=%async_computation.9 | async-start | bytes 8912896 | tf_op jit(solution)/shard_map/all_gather | solution.py:52
  443.6 185.9 %reduce-scatter.9.cloned.1.call-start = ((), (), s32[]{:S(2)}) async-start(), calls=%async_computation.10 | async-start | bytes 9437184 | tf_op jit(solution)/shard_map/reduce_scatter | solution.py:56
  539.3 160.2 %copy-start.3 = (bf16[64,512]{1,0:T(8,128)(2,1)S(1)}, bf16[64,512]{1,0:T(8,128)(2,1)}, u32[]{:S(2)}) copy-start(bf16[64,512]{1,0:T(8,128)(2,1)} %reduce-scatter.7.cloned.1.call-done) | copy-start | bytes 196612
  539.3 160.1 %reduce-scatter.11.cloned.1.call-start = ((), (), s32[]{:S(2)}) async-start(), calls=%async_computation.11 | async-start | bytes 1114112 | tf_op jit(solution)/shard_map/reduce_scatter | solution.py:59
Sparse Core Ops, SparseCore 0:
  79.6 73.9 all-gather.2
  217.9 89.5 reduce-scatter.4
  311.2 65.8 reduce-scatter.6
  443.7 75.0 all-gather.4
  539.4 90.0 reduce-scatter.8
  633.6 65.7 reduce-scatter.10

commit v2 on v1

v2 whole, which is shorter than its diff:
```python
import functools
import math

import jax
import jax.numpy as jnp
import numpy as np
from jax import lax
from jax.experimental import pallas as pl
from jax.experimental.pallas import tpu as pltpu
from jax.sharding import PartitionSpec as P


HEAD_DIM = 128
EPSILON = 1e-06
ROTARY_BASE = 1000000.0
TOKENS = 512
MODEL = 8192
BLOCK = 512
ROWS = 16
BF = jnp.bfloat16
F32 = jnp.float32
MESH = pl.DeviceIdType.MESH


def dot_nt(left, right):
    return lax.dot_general(left, right, (((1,), (1,)), ((), ())), preferred_element_type=F32)


def dot_nn(left, right):
    return lax.dot_general(left, right, (((1,), (0,)), ((), ())), preferred_element_type=F32)


GATHER = {
    "s1p": (0, 2, 1, 0, 512, 1, 1),
    "s1m": (0, 1, 1, 0, 512, 1, 3),
    "f1m": (1, 3, 1, 0, 256, 1, 3),
    "f1p": (2, 3, 1, 256, 256, 1, 1),
    "o2p": (0, 8, 1, 0, 512, 2, 1),
    "o2m": (0, 4, 1, 0, 512, 2, 3),
    "r2p": (1, 9, 3, 0, 512, 2, 1),
    "r2m": (1, 5, 3, 0, 512, 2, 3),
    "f2m": (4, 12, 2, 0, 512, 2, 3),
    "f2p": (10, 14, 2, 0, 512, 2, 1),
    "o3p": (0, 32, 1, 0, 512, 3, 1),
    "o3m": (0, 16, 1, 0, 512, 3, 3),
    "r3p": (1, 33, 3, 0, 512, 3, 1),
    "r3m": (1, 17, 3, 0, 512, 3, 3),
    "f3m0": (16, 48, 4, 0, 512, 3, 3),
    "f3m1": (20, 52, 4, 0, 512, 3, 3),
    "f3p2": (40, 56, 4, 0, 512, 3, 1),
    "f3p3": (44, 60, 4, 0, 512, 3, 1),
}
for _k in (1, 2, 3):
    GATHER[f"g3p{_k}"] = (4 * _k, 32 + 4 * _k, 4, 0, 512, 3, 1)
    GATHER[f"g3m{_k}"] = (4 * _k, 16 + 4 * _k, 4, 0, 512, 3, 3)
GATHER_ID = {name: i for i, name in enumerate(GATHER)}

SCATTER = {}
for _i, _k in enumerate((3, 2)):
    SCATTER[f"a3{_k}"] = (48 + 4 * _k, 4 * _i, 4, 0, 512, 3, 1)
for _i, _k in enumerate((1, 0)):
    SCATTER[f"b3{_k}"] = (48 + 4 * _k, 8 + 4 * _i, 4, 0, 512, 3, 3)
for _k in range(4):
    SCATTER[f"p3{_k}"] = (16 + 4 * _k, 16 + 4 * _k, 4, 0, 512, 3, 1)
    SCATTER[f"m3{_k}"] = (32 + 4 * _k, 32 + 4 * _k, 4, 0, 512, 3, 3)
SCATTER["a2"] = (14, 48, 2, 0, 512, 2, 1)
SCATTER["b2"] = (12, 50, 2, 0, 512, 2, 3)
SCATTER["p2"] = (4, 52, 4, 0, 512, 2, 1)
SCATTER["m2"] = (8, 56, 4, 0, 512, 2, 3)
SCATTER["a1"] = (3, 60, 1, 0, 256, 1, 1)
SCATTER["b1"] = (3, 60, 1, 256, 256, 1, 3)
SCATTER["p1"] = (1, 61, 1, 0, 512, 1, 1)
SCATTER["m1"] = (2, 62, 1, 0, 512, 1, 3)
SCATTER_ID = {name: i for i, name in enumerate(SCATTER)}


def one_hot3(value):
    second, third = lax.rem(value, 2), lax.div(value, 2)
    return 1 - second - third, second, third


def kernel(
    tok_ref, small_ref, wq_hbm, wkv_hbm, wo_hbm, wg_hbm, wu_hbm, wd_hbm,
    cosk_hbm, sink_hbm, cosq_hbm, sinq_hbm,
    out_ref,
    wq, wkv, wo, wg, wu, wd, cosk, sink, cosq, sinq,
    ag, xb, part, sb, rb, stats, kvall, att, hid, accq, acckv, accg, accu, resid,
    ag_send, ag_recv, px_send, px_recv, rs_send, rs_recv, st_send, st_recv,
    kv_send, kv_recv, kf_send, kf_recv, at_send, at_recv, hd_send, hd_recv,
    wl_sem, ws_sem, wr_sem, ol_sem, os_sem, or_sem, dl_sem, ds_sem, dr_sem,
):
    gx, gy = lax.axis_index("gx"), lax.axis_index("gy")
    x, y_lo = lax.rem(gx, 4), lax.div(gx, 4)
    core, z, y_hi = lax.rem(gy, 2), lax.rem(lax.div(gy, 2), 4), lax.div(gy, 8)
    y = y_hi * 2 + y_lo
    chip = y_hi * 4 + z
    partner = (gx, gy + 1 - 2 * core)

    def device(x, y, z):
        return (lax.rem(y, 2) * 4 + x, lax.div(y, 2) * 8 + z * 2 + core)

    def turn(v):
        group, item = lax.div(v, 2), lax.rem(v, 2)
        return (1 - group) * core * (1 + item) + group * (1 + item - core)

    def toward(v, level, sign):
        e0, e1, e2 = one_hot3(lax.rem(turn(v) + 3 - level, 3))
        return device(lax.rem(x + sign * e0, 4), lax.rem(y + sign * e1, 4), lax.rem(z + sign * e2, 4))

    def slot(position, mine):
        d = lax.rem(position - mine + 4, 4)
        return d + lax.div(d, 2) - 2 * lax.div(d, 3)

    def place(rotation, px, py, pz):
        e0, e1, e2 = one_hot3(rotation)
        return (
            (16 * e0 + e1 + 4 * e2) * slot(px, x)
            + (4 * e0 + 16 * e1 + e2) * slot(py, y)
            + (e0 + 4 * e1 + 16 * e2) * slot(pz, z)
        )

    def remote(src, dst, send, recv, target):
        return pltpu.make_async_remote_copy(
            src_ref=src, dst_ref=dst, send_sem=send, recv_sem=recv, device_id=target, device_id_type=MESH
        )

    barrier = pltpu.get_barrier_semaphore()
    greeted = [
        device(lax.rem(x + 1, 4), y, z), device(lax.rem(x + 3, 4), y, z),
        device(x, lax.rem(y + 1, 4), z), device(x, lax.rem(y + 3, 4), z),
    ] + [(gx, lax.rem(gy + d, 16)) for d in range(1, 16)]
    for target in greeted:
        pl.semaphore_signal(barrier, inc=1, device_id=target, device_id_type=MESH)

    whole = ((wq_hbm, wq), (wkv_hbm, wkv), (wg_hbm, wg), (wu_hbm, wu))
    tables = ((cosk_hbm, cosk), (sink_hbm, sink), (cosq_hbm, cosq), (sinq_hbm, sinq))
    local_copies = [
        pltpu.make_async_copy(src, dst.at[core], wl_sem.at[i]) for i, (src, dst) in enumerate(whole)
    ]
    table_copies = [
        pltpu.make_async_copy(src, dst, wl_sem.at[4 + i]) for i, (src, dst) in enumerate(tables)
    ]
    remote_copies = [
        remote(src, dst.at[core], ws_sem.at[i], wr_sem.at[i], partner) for i, (src, dst) in enumerate(whole)
    ]
    columns = lambda f, side: pl.ds(pl.multiple_of((2 * f + side) * BLOCK, BLOCK), BLOCK)
    out_local = [pltpu.make_async_copy(wo_hbm.at[:, columns(f, core)], wo.at[core, f], ol_sem.at[f]) for f in range(8)]
    down_local = [pltpu.make_async_copy(wd_hbm.at[:, columns(f, core)], wd.at[core, f], dl_sem.at[f]) for f in range(8)]
    out_remote = [remote(wo_hbm.at[:, columns(f, 1 - core)], wo.at[core, f], os_sem.at[f], or_sem.at[f], partner) for f in range(8)]
    down_remote = [remote(wd_hbm.at[:, columns(f, 1 - core)], wd.at[core, f], ds_sem.at[f], dr_sem.at[f], partner) for f in range(8)]
    for copy in local_copies[:2] + table_copies + out_local + local_copies[2:] + down_local:
        copy.start()

    def column_sums(squares):
        folded = squares[:, :128] + squares[:, 128:256] + squares[:, 256:384] + squares[:, 384:]
        return jnp.sum(jnp.transpose(folded), axis=0, keepdims=True)

    def share_stats(phase, values, extra):
        squares = column_sums(values * values)
        row = lax.broadcasted_iota(jnp.int32, (8, 128), 0)
        wide = jnp.concatenate([squares, jnp.zeros((1, 64), F32)], axis=1)
        tile = jnp.where(row == 0, wide, jnp.zeros((8, 128), F32))
        if extra is not None:
            tile = jnp.where(row == 1, extra, tile)
        stats[phase, 0] = tile

    def stat_copy(phase, d):
        return remote(
            stats.at[phase, 0], stats.at[phase, d], st_send.at[phase, d], st_recv.at[phase, d],
            (gx, lax.rem(gy + d, 16)),
        )

    def inverse_root(phase):
        total = jnp.sum(jnp.sum(stats[phase], axis=0), axis=0, keepdims=True) if False else None
        row = lax.broadcasted_iota(jnp.int32, (8, 128), 0)
        summed = jnp.sum(stats[phase], axis=0)
        total = jnp.sum(jnp.where(row == 0, summed, 0.0), axis=0, keepdims=True)[:, :64]
        inverse = lax.rsqrt(total / MODEL + EPSILON)
        tall = jnp.transpose(jnp.broadcast_to(inverse, (128, 64)))
        return jnp.concatenate([tall] * 4, axis=1)

    def normalize_into_gather(phase, values, gain):
        scaled = (values * inverse_root(phase) * gain).astype(BF)
        for u in range(4):
            ag[lax.rem(u + 2 * core, 4), 0] = scaled[16 * u : 16 * u + 16]

    def gather_copy(name, v):
        src, dst, count, col, width, level, sign = GATHER[name]
        i = GATHER_ID[name]
        if width == 512:
            a, b = ag.at[v, pl.ds(src, count)], ag.at[v, pl.ds(dst, count)]
        else:
            a, b = ag.at[v, src, :, pl.ds(col, width)], ag.at[v, dst, :, pl.ds(col, width)]
        return remote(a, b, ag_send.at[v, i], ag_recv.at[v, i], toward(v, level, sign))

    def px_copy(j, k):
        return remote(
            ag.at[2 + j, pl.ds(16 * k, 16)], xb.at[j, pl.ds(16 * k, 16)], px_send.at[j, k], px_recv.at[j, k], partner
        )

    def units(body, first=0, last=4):
        @pl.loop(first, last)
        def _(v):
            body(v)

    def gather():
        start = lambda v, *names: [gather_copy(n, v).start() for n in names]
        arrive = lambda v, *names: [gather_copy(n, v).wait_recv() for n in names]

        def t0(v):
            start(v, "s1p", "s1m", "o2p", "o2m", "o3p", "o3m")

        def t1(v):
            arrive(v, "s1m")
            start(v, "f1m")
            arrive(v, "s1p")
            start(v, "f1p")

        def t2(v):
            arrive(v, "f1m", "f1p")
            start(v, "r2p", "r2m", "r3p", "r3m")

        def t3(v):
            arrive(v, "o2m", "r2m")
            start(v, "f2m", "g3p1", "g3m1")
            arrive(v, "o2p", "r2p")
            start(v, "f2p", "g3p2", "g3m2")

        def t4(v):
            arrive(v, "o3m", "r3m")
            start(v, "f3m0")

        def t5(v):
            arrive(v, "f2m", "f2p")
            start(v, "g3p3", "g3m3")

        def t6(v):
            arrive(v, "g3m1")
            start(v, "f3m1")
            arrive(v, "o3p", "r3p", "g3p1", "g3p2")
            start(v, "f3p2")

        def t7(v):
            arrive(v, "g3p3")
            start(v, "f3p3")
            arrive(v, "g3m2", "g3m3")

        def t8(v):
            arrive(v, "f3m0", "f3m1", "f3p2", "f3p3")

        for step in (t0, t1, t2, t3, t4, t5):
            units(step)
        for j in range(2):
            px_copy(j, 0).start()
        units(t6)
        units(t7, 2, 4)
        for j in range(2):
            px_copy(j, 1).start()
            px_copy(j, 2).start()
        units(t7, 0, 2)
        units(t8, 2, 4)
        for j in range(2):
            px_copy(j, 3).start()
        units(t8, 0, 2)
        for j in range(2):
            for k in range(4):
                px_copy(j, k).wait_recv()

    def gather_drain():
        units(lambda v: [gather_copy(n, v).wait_send() for n in GATHER])
        for j in range(2):
            for k in range(4):
                px_copy(j, k).wait_send()

    def gathered(f, mine):
        fy, fz = lax.div(f, 4), lax.rem(f, 4)
        pieces = []
        for j in range(2):
            rotation = turn(j) if mine else j + core
            for ty in range(2):
                for tx in range(4):
                    at = place(rotation, tx, fy * 2 + ty, fz)
                    pieces.append(ag[j, at] if mine else xb[j, at])
        return jnp.concatenate(pieces, axis=0)

    def feature_columns(f, mine):
        return columns(f, core if mine else 1 - core)

    def scatter_copy(name, v):
        src, dst, count, col, width, level, sign = SCATTER[name]
        i = SCATTER_ID[name]
        if width == 512:
            a, b = sb.at[v, pl.ds(src, count)], rb.at[v, pl.ds(dst, count)]
        else:
            a, b = sb.at[v, src, :, pl.ds(col, width)], rb.at[v, dst, :, pl.ds(col, width)]
        return remote(a, b, rs_send.at[v, i], rs_recv.at[v, i], toward(v, level, sign))

    def rs_start(v, *names):
        for n in names:
            scatter_copy(n, v).start()

    def rs_arrive(v, *names):
        for n in names:
            scatter_copy(n, v).wait_recv()

    def cast(v, src, count=4):
        sb[v, pl.ds(src, count)] = part[v, pl.ds(src, count)].astype(BF)

    def cast_sum(v, src, place_at, count=4):
        sb[v, pl.ds(src, count)] = (
            part[v, pl.ds(src, count)] + rb[v, pl.ds(place_at, count)].astype(F32)
        ).astype(BF)

    def scatter_first(v):
        for k in (3, 2):
            cast(v, 48 + 4 * k)
            rs_start(v, f"a3{k}")
        for k in (1, 0):
            cast(v, 48 + 4 * k)
            rs_start(v, f"b3{k}")
        for k in (3, 2):
            cast(v, 32 + 4 * k)
            rs_start(v, f"m3{k}")

    def scatter_rest():
        def s1(v):
            for k in (3, 2):
                rs_arrive(v, f"a3{k}")
                cast_sum(v, 16 + 4 * k, 4 * (3 - k))
                rs_start(v, f"p3{k}")
            for k in (1, 0):
                cast(v, 16 + 4 * k)
                rs_start(v, f"p3{k}")
                rs_arrive(v, f"b3{k}")
                cast_sum(v, 32 + 4 * k, 8 + 4 * (1 - k))
                rs_start(v, f"m3{k}")

        def total3(v, k):
            rs_arrive(v, f"m3{k}", f"p3{k}")
            return (
                part[v, pl.ds(4 * k, 4)]
                + rb[v, pl.ds(16 + 4 * k, 4)].astype(F32)
                + rb[v, pl.ds(32 + 4 * k, 4)].astype(F32)
            )

        def s2(v):
            sb[v, pl.ds(12, 4)] = total3(v, 3).astype(BF)
            rs_start(v, "a2", "b2")

        def s3(v):
            total = total3(v, 2)
            rs_arrive(v, "b2")
            sb[v, pl.ds(8, 2)] = (total[:2] + rb[v, pl.ds(50, 2)].astype(F32)).astype(BF)
            sb[v, pl.ds(10, 2)] = total[2:].astype(BF)
            rs_start(v, "m2")
            total = total3(v, 1)
            rs_arrive(v, "a2")
            sb[v, pl.ds(6, 2)] = (total[2:] + rb[v, pl.ds(48, 2)].astype(F32)).astype(BF)
            sb[v, pl.ds(4, 2)] = total[:2].astype(BF)
            rs_start(v, "p2")

        def s4(v):
            total = total3(v, 0)
            rs_arrive(v, "m2", "p2")
            total = total + rb[v, pl.ds(52, 4)].astype(F32) + rb[v, pl.ds(56, 4)].astype(F32)
            part[v, pl.ds(0, 4)] = total
            sb[v, 3] = total[3].astype(BF)
            rs_start(v, "a1", "b1")

        def s5(v):
            sb[v, 1, :, 256:] = part[v, 1, :, 256:].astype(BF)
            rs_arrive(v, "a1")
            sb[v, 1, :, :256] = (part[v, 1, :, :256] + rb[v, 60, :, :256].astype(F32)).astype(BF)
            rs_start(v, "p1")
            sb[v, 2, :, :256] = part[v, 2, :, :256].astype(BF)
            rs_arrive(v, "b1")
            sb[v, 2, :, 256:] = (part[v, 2, :, 256:] + rb[v, 60, :, 256:].astype(F32)).astype(BF)
            rs_start(v, "m1")

        def s6(v):
            rs_arrive(v, "m1", "p1")
            part[v, 0] = part[v, 0] + rb[v, 61].astype(F32) + rb[v, 62].astype(F32)

        for step in (s1, s2, s3, s4, s5, s6):
            units(step)
        units(lambda v: [scatter_copy(n, v).wait_send() for n in SCATTER])

    def scattered():
        return jnp.concatenate([part[lax.rem(u + 2 * core, 4), 0] for u in range(4)], axis=0)

    def spread(pair, f, product):
        fy, fz = lax.div(f, 4), lax.rem(f, 4)
        for j in range(2):
            for ty in range(2):
                for tx in range(4):
                    at = place(turn(2 * pair + j), tx, fy * 2 + ty, fz)
                    row = 128 * j + 64 * ty + 16 * tx
                    part[2 * pair + j, at] = product[row : row + 16]

    tokens = tok_ref[...].astype(F32)
    share_stats(0, tokens, small_ref[:, 2176:2304])
    pl.semaphore_wait(barrier, len(greeted))
    for d in range(1, 16):
        stat_copy(0, d).start()
    for copy in remote_copies[:2]:
        copy.start()
    for d in range(1, 16):
        stat_copy(0, d).wait_recv()
    normalize_into_gather(0, tokens, small_ref[:, :512])
    documents = jnp.sum(
        jnp.where(lax.broadcasted_iota(jnp.int32, (16, 8, 128), 1) == 1, stats[0], 0.0), axis=1
    )
    for copy in out_remote + remote_copies[2:] + down_remote:
        copy.start()
    for copy in local_copies[:2] + table_copies:
        copy.wait()
    for copy in remote_copies[:2]:
        copy.wait_recv()
    gather()

    acckv[...] = jnp.zeros_like(acckv)

    @pl.loop(0, 8)
    def _(f):
        for mine in (True, False):
            cols = feature_columns(f, mine)
            weights = jnp.concatenate([wkv[0, :, cols], wkv[1, :, cols]], axis=0)
            acckv[...] += dot_nt(weights, gathered(f, mine))

    kv_sum = acckv[...]
    kvall[core, chip] = jnp.concatenate([kv_sum[0:8], kv_sum[16:24], kv_sum[8:16], kv_sum[24:32]], axis=0)

    def kv_copy(d):
        there = lax.rem(gy + 2 * d, 16)
        return remote(kvall.at[core, chip], kvall.at[core, chip], kv_send.at[d], kv_recv.at[d], (gx, there))

    def kv_arrival(d):
        source = lax.rem(chip + 8 - d, 8)
        return remote(kvall.at[core, source], kvall.at[core, source], kv_send.at[d], kv_recv.at[d], partner)

    for d in range(1, 8):
        kv_copy(d).start()

    accq[...] = jnp.zeros_like(accq)

    @pl.loop(0, 8)
    def _(f):
        for mine in (True, False):
            cols = feature_columns(f, mine)
            weights = jnp.concatenate([wq[0, :, cols], wq[1, :, cols]], axis=0)
            accq[...] += dot_nt(gathered(f, mine), weights)

    bias_at = pl.ds(pl.multiple_of(1024 + 128 * chip, 128), 128)
    query = accq[...] + small_ref[:, bias_at]
    own_rows = pl.ds(pl.multiple_of(256 * core, 256), 256)
    turned = jnp.concatenate([query[:, 64:], query[:, :64]], axis=1)
    queries = (query * cosq[own_rows, :] + turned * sinq[own_rows, :]).astype(BF)

    for d in range(1, 8):
        kv_arrival(d).wait_recv()
    forward = remote(kvall.at[core], kvall.at[core], kf_send, kf_recv, partner)
    forward.start()

    def token_parts(index, own_core):
        item, low, along, row = (
            (index >> 7) & 1, (index >> 6) & 1, (index >> 4) & 3, index & 15,
        )
        return 256 * low + 64 * along + 32 * own_core + 16 * item + row, 8 * low + 2 * along + own_core, 16 * item + row

    def owner(index):
        held = gy - index
        return jnp.where(held < 0, held + 16, held)

    docs = documents.astype(BF)
    key_index = lax.broadcasted_iota(jnp.int32, (128, 512), 1)
    _, _, key_lane = token_parts(key_index, key_index >> 8)
    pick = jnp.where(lax.broadcasted_iota(jnp.int32, (128, 512), 0) == key_lane, 1.0, 0.0).astype(BF)
    key_docs = dot_nn(docs, pick)
    key_index = lax.broadcasted_iota(jnp.int32, (16, 512), 1)
    _, key_owner, _ = token_parts(key_index, key_index >> 8)
    is_owner = owner(lax.broadcasted_iota(jnp.int32, (16, 512), 0)) == key_owner
    key_docs = jnp.sum(jnp.where(is_owner, key_docs, 0.0), axis=0, keepdims=True)
    query_index = lax.broadcasted_iota(jnp.int32, (256, 128), 0)
    _, _, query_lane = token_parts(query_index, core)
    pick = jnp.where(lax.broadcasted_iota(jnp.int32, (256, 128), 1) == query_lane, 1.0, 0.0).astype(BF)
    query_docs = dot_nt(pick, docs)
    query_index = lax.broadcasted_iota(jnp.int32, (256, 16), 0)
    _, query_owner, _ = token_parts(query_index, core)
    is_owner = owner(lax.broadcasted_iota(jnp.int32, (256, 16), 1)) == query_owner
    query_docs = jnp.sum(jnp.where(is_owner, query_docs, 0.0), axis=1, keepdims=True)
    key_index = lax.broadcasted_iota(jnp.int32, (256, 512), 1)
    key_position, _, _ = token_parts(key_index, key_index >> 8)
    query_position, _, _ = token_parts(lax.broadcasted_iota(jnp.int32, (256, 512), 0), core)
    allowed = (key_position <= query_position) & (key_docs == query_docs)

    value_bias = jnp.transpose(jnp.broadcast_to(small_ref[:, 2048:2176], (128, 128)))
    value_bias = jnp.concatenate([value_bias] * 2, axis=1)
    remote(kvall.at[1 - core], kvall.at[1 - core], kf_send, kf_recv, partner).wait_recv()
    key_parts, value_parts = [], []
    for side in range(2):
        held = kvall[side]
        keys = held[:, :16].reshape(128, 256)
        first, second = keys[:64], keys[64:]
        cosine, sine = cosk[:, 256 * side : 256 * side + 256], sink[:, 256 * side : 256 * side + 256]
        key_parts.append(
            jnp.concatenate([first * cosine - second * sine, second * cosine + first * sine], axis=0).astype(BF)
        )
        value_parts.append((held[:, 16:].reshape(128, 256) + value_bias).astype(BF))
    keys = jnp.concatenate(key_parts, axis=1)
    values = jnp.concatenate(value_parts, axis=1)
    scores = dot_nn(queries, keys) / math.sqrt(HEAD_DIM)
    scores = jnp.where(allowed, scores, -jnp.inf)
    weights = jnp.where(allowed, jnp.exp(scores - jnp.max(scores, axis=1, keepdims=True)), 0.0)
    denominator = jnp.sum(weights, axis=1, keepdims=True)
    att[0] = (dot_nt(weights.astype(BF), values) / denominator).astype(BF)
    send_att = remote(att.at[0], att.at[1], at_send, at_recv, partner)
    send_att.start()

    for copy in out_local:
        copy.wait()
    for copy in out_remote:
        copy.wait_recv()
    for pair in range(2):
        if pair == 1:
            send_att.wait_recv()

        @pl.loop(0, 8)
        def _(f):
            weights = jnp.concatenate([wo[0, f], wo[1, f]], axis=0)
            spread(pair, f, dot_nn(att[pair], weights))

        units(scatter_first, 2 * pair, 2 * pair + 2)
    gather_drain()
    scatter_rest()

    resid[...] = (tok_ref[...].astype(F32) + scattered()).astype(BF)

    values = resid[...].astype(F32)
    share_stats(1, values, None)
    for d in range(1, 16):
        stat_copy(1, d).start()
    for copy in local_copies[2:]:
        copy.wait()
    for copy in remote_copies[2:]:
        copy.wait_recv()
    for d in range(1, 16):
        stat_copy(1, d).wait_recv()
    normalize_into_gather(1, values, small_ref[:, 512:1024])
    gather()

    accg[...] = jnp.zeros_like(accg)
    accu[...] = jnp.zeros_like(accu)

    @pl.loop(0, 8)
    def _(f):
        for mine in (True, False):
            cols = feature_columns(f, mine)
            block = gathered(f, mine)
            for side in range(2):
                accg[side] += dot_nt(block, wg[side, :, cols])
                accu[side] += dot_nt(block, wu[side, :, cols])

    for side in range(2):
        gate = accg[side]
        hid[0, side] = (gate / (1.0 + jnp.exp(-gate)) * accu[side]).astype(BF)
    send_hid = remote(hid.at[0], hid.at[1], hd_send, hd_recv, partner)
    send_hid.start()
    for copy in down_local:
        copy.wait()
    for copy in down_remote:
        copy.wait_recv()
    for pair in range(2):
        if pair == 1:
            send_hid.wait_recv()

        @pl.loop(0, 8)
        def _(f):
            product = dot_nn(hid[pair, 0], wd[0, f]) + dot_nn(hid[pair, 1], wd[1, f])
            spread(pair, f, product)

        units(scatter_first, 2 * pair, 2 * pair + 2)
    gather_drain()
    scatter_rest()
    out_ref[...] = (resid[...].astype(F32) + scattered()).astype(BF)

    for d in range(1, 16):
        stat_copy(0, d).wait_send()
        stat_copy(1, d).wait_send()
    for d in range(1, 8):
        kv_copy(d).wait_send()
    forward.wait_send()
    send_att.wait_send()
    send_hid.wait_send()
    for copy in remote_copies + out_remote + down_remote:
        copy.wait_send()


def rotary_tables():
    half = HEAD_DIM // 2
    frequency = np.power(np.float32(ROTARY_BASE), -(np.arange(half, dtype=np.float32) * 2.0) / HEAD_DIM).astype(np.float32)
    index = np.arange(TOKENS)
    side, item, low, along, row = index >> 8, (index >> 7) & 1, (index >> 6) & 1, (index >> 4) & 3, index & 15
    position = 256 * low + 64 * along + 32 * side + 16 * item + row
    angles = (position.astype(np.float32)[:, None] * frequency[None, :]).astype(np.float32)
    cosine, sine = np.cos(angles).astype(np.float32), np.sin(angles).astype(np.float32)
    return (
        np.ascontiguousarray(cosine.T), np.ascontiguousarray(sine.T),
        np.concatenate([cosine, cosine], axis=1), np.concatenate([-sine, sine], axis=1),
    )


def shards(
    tokens, segment_ids, attn_gain, query_weight, query_bias, key_weight, value_weight, value_bias,
    out_weight, ffn_gain, gate_weight, up_weight, down_weight,
):
    small = jnp.concatenate(
        [
            attn_gain.astype(F32), ffn_gain.astype(F32), query_bias.astype(F32), value_bias.astype(F32),
            segment_ids.astype(F32), jnp.zeros((96,), F32),
        ]
    )[None, :]
    kv_weight = jnp.concatenate([key_weight, value_weight], axis=0)
    units = gate_weight.shape[0]
    any_spec = pl.BlockSpec(memory_space=pl.ANY)
    vmem_spec = pl.BlockSpec(memory_space=pltpu.VMEM)
    dma = pltpu.SemaphoreType.DMA
    gathers, scatters = len(GATHER), len(SCATTER)
    return pl.pallas_call(
        kernel,
        out_shape=jax.ShapeDtypeStruct((64, BLOCK), BF),
        in_specs=[vmem_spec] * 2 + [any_spec] * 10,
        out_specs=vmem_spec,
        scratch_shapes=[
            pltpu.VMEM((2, 64, MODEL), BF),
            pltpu.VMEM((2, 16, MODEL), BF),
            pltpu.VMEM((2, 8, 64, BLOCK), BF),
            pltpu.VMEM((2, units, MODEL), BF),
            pltpu.VMEM((2, units, MODEL), BF),
            pltpu.VMEM((2, 8, units, BLOCK), BF),
            pltpu.VMEM((64, 512), F32),
            pltpu.VMEM((64, 512), F32),
            pltpu.VMEM((512, 128), F32),
            pltpu.VMEM((512, 128), F32),
            pltpu.VMEM((4, 64, ROWS, BLOCK), BF),
            pltpu.VMEM((2, 64, ROWS, BLOCK), BF),
            pltpu.VMEM((4, 64, ROWS, BLOCK), F32),
            pltpu.VMEM((4, 64, ROWS, BLOCK), BF),
            pltpu.VMEM((4, 63, ROWS, BLOCK), BF),
            pltpu.VMEM((2, 16, 8, 128), F32),
            pltpu.VMEM((2, 8, 32, 256), F32),
            pltpu.VMEM((2, 256, 128), BF),
            pltpu.VMEM((2, 2, 256, units), BF),
            pltpu.VMEM((256, 128), F32),
            pltpu.VMEM((32, 256), F32),
            pltpu.VMEM((2, 256, units), F32),
            pltpu.VMEM((2, 256, units), F32),
            pltpu.VMEM((64, BLOCK), BF),
            dma((4, gathers)), dma((4, gathers)),
            dma((2, 4)), dma((2, 4)),
            dma((4, scatters)), dma((4, scatters)),
            dma((2, 16)), dma((2, 16)),
            dma((8,)), dma((8,)),
            dma, dma, dma, dma, dma, dma,
            dma((8,)), dma((4,)), dma((4,)),
            dma((8,)), dma((8,)), dma((8,)),
            dma((8,)), dma((8,)), dma((8,)),
        ],
        compiler_params=pltpu.CompilerParams(
            collective_id=0, has_side_effects=True, vmem_limit_bytes=60 * 1024 * 1024
        ),
        name="layer",
    )(
        tokens, small, query_weight, kv_weight, out_weight, gate_weight, up_weight, down_weight, *rotary_tables()
    )


def solution(mesh):
    placed = (
        P("gx", "gy"),
        P("gy"),
        P("gy"),
        P(("gx", "gy"), None),
        P("gx"),
        P(("gx", "gy"), None),
        P(("gx", "gy"), None),
        P("gx"),
        P(("gx", "gy"), None),
        P("gy"),
        P(("gx", "gy"), None),
        P(("gx", "gy"), None),
        P(("gx", "gy"), None),
    )
    return jax.shard_map(
        shards, mesh=mesh, in_specs=placed, out_specs=P("gx", "gy"), check_vma=False
    )
```

time: 708 us -> 162 us (0.23)
  waiting for transfers between devices: 455 us -> 0 us
  blocking collectives: 180 us -> 0 us
  Pallas kernels: 0 us -> 155 us
  matrix products: 40.9 us -> 0 us
  between operations: 14.4 us -> 0.01 us
  other arithmetic: 9.96 us -> 2.33 us
    reduce_scatter x4 -> x0, waiting for transfers between devices: 319 us -> none  [the longest x2 180 us: scatter_sum(): lax.psum_scatter(partial.astype(jnp.bfloat16), 'gx', scatter_dimension=0,...]
    pallas_call x0 -> x1, Pallas kernels: none -> 155 us  [shards(): pl.pallas_call(kernel, out_shape=jax.ShapeDtypeStruct((64, BLOCK), BF), i...]
    all_gather x2 -> x0, waiting for transfers between devices: 135 us -> none  [normalize(): return lax.all_gather(by_row, 'gy', axis=1, tiled=True)]
    all_gather x3 -> x0, blocking collectives: 87.9 us -> none  [the longest x2 62 us: normalize(): by_row = lax.all_gather(normed, 'gx', axis=0, tiled=True)]
    psum x2 -> x0, blocking collectives: 72.7 us -> none  [normalize(): squares = lax.psum(jnp.sum(floats * floats, axis=1), 'gy')]
    dot_general x7 -> x0, matrix products: 40.5 us -> none  [the longest x4 20.8 us: project_rows(): lax.dot_general(row_block, weight_rows, (((1,), (1,)), ((), ())), preferr...]
    all_to_all x1 -> x0, blocking collectives: 10.2 us -> none  [shards(): lax.all_to_all(attended, 'gy', split_axis=1, concat_axis=0, tiled=True)]
    unnamed x1 -> x0, blocking collectives: 8.91 us -> none
  transfers between devices with their start and end apart: 7 -> 0, of which waited for: 6 -> 0; matrix products, arithmetic and copies ran while one was open for 2% -> 0% of each run, Pallas kernels for 0% -> 0%
where the time goes in v2:
time: 162 us
  Pallas kernels  155 us (96%)
  local copies, waits for them, and re-layouts  4.88 us (3%)
  other arithmetic  2.33 us (1%)
    pallas_call x1, Pallas kernels, shards(): pl.pallas_call(kernel, out_shape=jax.ShapeDtypeStruct((64, BLOCK), BF), i...  155 us

profile of v2, /device:TPU:0, one launch (start us, length us, event | category | flops | bytes accessed | tf_op | source)
XLA Modules:
  0.0 162.0 jit_solution(3739029042550203702)
XLA Ops:
  0.0 0.7 convert_element_type.19
  0.7 2.8 %concatenate.6 = f32[2304]{0:T(1024)S(1)} concatenate(bf16[512]{0:T(512)(128)(2,1)} %param.19, bf16[512]{0:T(512)(128)(2,1)} %param.26, bf16[1024]{0:T(1024)(128)(2,1)} %param.21, bf16[128]{0:T(256)(128)(2,1)} %param.24, f32[32]{0:T(128)S(1)} %convert_element_type.19, f32[96]{0:T(128)S(1)} %broadcast_in_dim.6), dimensions={0} | concatenate | bytes 14080 | tf_op jit(solution)/shard_map/concatenate | solution.py:616
  3.5 0.6 broadcast_in_dim.7.small_ref
  4.1 1.7 %pad_maximum_fusion.wkv_hbm = bf16[16,8192]{1,0:T(8,128)(2,1)} fusion(bf16[8,8192]{1,0:T(8,128)(2,1)} %param.23, bf16[8,8192]{1,0:T(8,128)(2,1)} %param.22), kind=kLoop, calls=%fused_computation | loop fusion | flops 524288 | bytes 524288 | tf_op jit(solution)/shard_map/concatenate | solution.py:622
  5.7 154.8 %layer.1 = bf16[64,512]{1,0:T(8,128)(2,1)} custom-call(bf16[64,512]{1,0:T(8,128)(2,1)} %tok_ref.1, f32[1,2304]{1,0:T(1,128)} %broadcast_in_dim.7.small_ref, bf16[64,8192]{1,0:T(8,128)(2,1)} %wq_hbm.1, bf16[16,8192]{1,0:T(8,128)(2,1)} %pad_maximum_fusion.wkv_hbm, bf16[64,8192]{1,0:T(8,128)(2,1)} %wo_hbm.1, bf16[231,8192]{1,0:T(8,128)(2,1)} %wg_hbm.1, ...), custom_call_target="tpu_custom_call" | custom-call | tf_op jit(solution)/shard_map/layer/pallas_call | solution.py:628
  160.5 1.5 copy.19
  (1 shorter events, 0.0 us)

commit v3 on v2

--- a/solution.py
+++ b/solution.py
@@ -84,8 +84,8 @@
     cosk_hbm, sink_hbm, cosq_hbm, sinq_hbm,
     out_ref,
     wq, wkv, wo, wg, wu, wd, cosk, sink, cosq, sinq,
-    ag, xb, part, sb, rb, stats, kvall, att, hid, accq, acckv, accg, accu, resid,
-    ag_send, ag_recv, px_send, px_recv, rs_send, rs_recv, st_send, st_recv,
+    ag, xb, an, part, sb, rb, stats, sums, roots, tall, scale, kvall, att, hid, accq, acckv, accg, accu, resid,
+    ag_send, ag_recv, px_send, px_recv, rs_send, rs_recv, st_send, st_recv, su_send, su_recv, ro_send, ro_recv,
     kv_send, kv_recv, kf_send, kf_recv, at_send, at_recv, hd_send, hd_recv,
     wl_sem, ws_sem, wr_sem, ol_sem, os_sem, or_sem, dl_sem, ds_sem, dr_sem,
 ):
@@ -103,21 +103,34 @@
         group, item = lax.div(v, 2), lax.rem(v, 2)
         return (1 - group) * core * (1 + item) + group * (1 + item - core)
 
-    def toward(v, level, sign):
+    def neighbour(v, level, sign):
         e0, e1, e2 = one_hot3(lax.rem(turn(v) + 3 - level, 3))
         return device(lax.rem(x + sign * e0, 4), lax.rem(y + sign * e1, 4), lax.rem(z + sign * e2, 4))
+
+    neighbours = {
+        (v, level, sign): neighbour(v, level, sign) for v in range(4) for level in (1, 2, 3) for sign in (1, 3)
+    }
+
+    def toward(v, level, sign):
+        return neighbours[v, level, sign]
 
     def slot(position, mine):
         d = lax.rem(position - mine + 4, 4)
         return d + lax.div(d, 2) - 2 * lax.div(d, 3)
 
-    def place(rotation, px, py, pz):
+    def strides(rotation):
         e0, e1, e2 = one_hot3(rotation)
-        return (
-            (16 * e0 + e1 + 4 * e2) * slot(px, x)
-            + (4 * e0 + 16 * e1 + e2) * slot(py, y)
-            + (e0 + 4 * e1 + 16 * e2) * slot(pz, z)
-        )
+        return 16 * e0 + e1 + 4 * e2, 4 * e0 + 16 * e1 + e2, e0 + 4 * e1 + 16 * e2
+
+    x_slots = [slot(position, x) for position in range(4)]
+    unit_strides = [strides(turn(v)) for v in range(4)]
+    other_strides = [strides(j + core) for j in range(2)]
+
+    def places(stride, f):
+        fy, fz = lax.div(f, 4), lax.rem(f, 4)
+        z_part = stride[2] * slot(fz, z)
+        y_parts = [stride[1] * slot(fy * 2 + ty, y) + z_part for ty in range(2)]
+        return [y_parts[ty] + stride[0] * x_slots[tx] for ty in range(2) for tx in range(4)]
 
     def remote(src, dst, send, recv, target):
         return pltpu.make_async_remote_copy(
@@ -125,10 +138,11 @@
         )
 
     barrier = pltpu.get_barrier_semaphore()
-    greeted = [
-        device(lax.rem(x + 1, 4), y, z), device(lax.rem(x + 3, 4), y, z),
-        device(x, lax.rem(y + 1, 4), z), device(x, lax.rem(y + 3, 4), z),
-    ] + [(gx, lax.rem(gy + d, 16)) for d in range(1, 16)]
+    greeted = (
+        [device(x, lax.rem(y + 3 + 2 * y_lo, 4), z)]
+        + [(lax.rem(gx + e, 8), gy) for e in range(1, 8)]
+        + [(gx, lax.rem(gy + d, 16)) for d in range(1, 16)]
+    )
     for target in greeted:
         pl.semaphore_signal(barrier, inc=1, device_id=target, device_id_type=MESH)
 
@@ -151,38 +165,54 @@
     for copy in local_copies[:2] + table_copies + out_local + local_copies[2:] + down_local:
         copy.start()
 
-    def column_sums(squares):
+    def token_unit(v):
+        return pl.ds(pl.multiple_of(16 * lax.rem(v + 2 * core, 4), 16), 16)
+
+    def square_row(values):
+        squares = values * values
         folded = squares[:, :128] + squares[:, 128:256] + squares[:, 256:384] + squares[:, 384:]
-        return jnp.sum(jnp.transpose(folded), axis=0, keepdims=True)
-
-    def share_stats(phase, values, extra):
-        squares = column_sums(values * values)
-        row = lax.broadcasted_iota(jnp.int32, (8, 128), 0)
-        wide = jnp.concatenate([squares, jnp.zeros((1, 64), F32)], axis=1)
-        tile = jnp.where(row == 0, wide, jnp.zeros((8, 128), F32))
-        if extra is not None:
-            tile = jnp.where(row == 1, extra, tile)
-        stats[phase, 0] = tile
+        row = jnp.sum(jnp.transpose(folded), axis=0, keepdims=True)
+        return jnp.concatenate([row, jnp.zeros((1, 64), F32)], axis=1)
 
     def stat_copy(phase, d):
+        there = (gx, lax.rem(gy + d, 16))
+        if phase == 0:
+            return remote(stats.at[0], stats.at[d], st_send.at[d], st_recv.at[d], there)
+        return remote(sums.at[0], sums.at[d], su_send.at[d], su_recv.at[d], there)
+
+    def root_copy(phase, e):
         return remote(
-            stats.at[phase, 0], stats.at[phase, d], st_send.at[phase, d], st_recv.at[phase, d],
-            (gx, lax.rem(gy + d, 16)),
+            roots.at[phase, 0], roots.at[phase, e], ro_send.at[phase, e], ro_recv.at[phase, e], (lax.rem(gx + e, 8), gy)
         )
 
-    def inverse_root(phase):
-        total = jnp.sum(jnp.sum(stats[phase], axis=0), axis=0, keepdims=True) if False else None
-        row = lax.broadcasted_iota(jnp.int32, (8, 128), 0)
-        summed = jnp.sum(stats[phase], axis=0)
-        total = jnp.sum(jnp.where(row == 0, summed, 0.0), axis=0, keepdims=True)[:, :64]
-        inverse = lax.rsqrt(total / MODEL + EPSILON)
-        tall = jnp.transpose(jnp.broadcast_to(inverse, (128, 64)))
-        return jnp.concatenate([tall] * 4, axis=1)
-
-    def normalize_into_gather(phase, values, gain):
-        scaled = (values * inverse_root(phase) * gain).astype(BF)
-        for u in range(4):
-            ag[lax.rem(u + 2 * core, 4), 0] = scaled[16 * u : 16 * u + 16]
+    def spread_roots(phase):
+        for d in range(1, 16):
+            stat_copy(phase, d).wait_recv()
+        summed = jnp.sum(stats[:, :8] if phase == 0 else sums[...], axis=0)
+        inverse = lax.rsqrt(summed / MODEL + EPSILON)
+        roots[phase, 0] = inverse
+        for e in range(1, 8):
+            root_copy(phase, e).start()
+
+    def collect_roots(phase):
+        for e in range(1, 8):
+            root_copy(phase, e).wait_recv()
+        factors = jnp.concatenate([roots[phase, e, :1] for e in range(8)], axis=0)
+        tall[...] = jnp.transpose(jnp.concatenate([factors] * 16, axis=0))
+        lane = lax.broadcasted_iota(jnp.int32, (16, 128), 1)
+        for j in range(2):
+            rows = tall[pl.ds(pl.multiple_of(32 * core + 16 * j, 16), 16), :]
+            for owner_gx in range(8):
+                column = jnp.sum(jnp.where(lane == lax.rem(gx + 8 - owner_gx, 8), rows, 0.0), axis=1, keepdims=True)
+                scale[128 * j + 16 * owner_gx : 128 * j + 16 * owner_gx + 16] = jnp.broadcast_to(column, (16, 128))
+
+    def normalized(f, mine, first_row):
+        block = gathered(f, mine).astype(F32)
+        held = lax.rem(gy + 16 - (2 * f + (core if mine else 1 - core)), 16)
+        gains = stats[held, first_row : first_row + 4]
+        gain = jnp.concatenate([gains[i : i + 1] for i in range(4)], axis=1)
+        factor = scale[...]
+        return (block * jnp.concatenate([factor] * 4, axis=1) * gain).astype(BF)
 
     def gather_copy(name, v):
         src, dst, count, col, width, level, sign = GATHER[name]
@@ -199,16 +229,16 @@
         )
 
     def units(body, first=0, last=4):
-        @pl.loop(first, last)
-        def _(v):
+        for v in range(first, last):
             body(v)
 
-    def gather():
+    def gather_begin(v):
+        for name in ("s1p", "s1m", "o2p", "o2m", "o3p", "o3m"):
+            gather_copy(name, v).start()
+
+    def gather(beside):
         start = lambda v, *names: [gather_copy(n, v).start() for n in names]
         arrive = lambda v, *names: [gather_copy(n, v).wait_recv() for n in names]
-
-        def t0(v):
-            start(v, "s1p", "s1m", "o2p", "o2m", "o3p", "o3m")
 
         def t1(v):
             arrive(v, "s1m")
@@ -248,8 +278,9 @@
         def t8(v):
             arrive(v, "f3m0", "f3m1", "f3p2", "f3p3")
 
-        for step in (t0, t1, t2, t3, t4, t5):
+        for i, step in enumerate((t1, t2, t3, t4, t5)):
             units(step)
+            beside(i)
         for j in range(2):
             px_copy(j, 0).start()
         units(t6)
@@ -273,14 +304,10 @@
                 px_copy(j, k).wait_send()
 
     def gathered(f, mine):
-        fy, fz = lax.div(f, 4), lax.rem(f, 4)
         pieces = []
         for j in range(2):
-            rotation = turn(j) if mine else j + core
-            for ty in range(2):
-                for tx in range(4):
-                    at = place(rotation, tx, fy * 2 + ty, fz)
-                    pieces.append(ag[j, at] if mine else xb[j, at])
+            for at in places(unit_strides[j] if mine else other_strides[j], f):
+                pieces.append(ag[j, at] if mine else xb[j, at])
         return jnp.concatenate(pieces, axis=0)
 
     def feature_columns(f, mine):
@@ -322,7 +349,7 @@
             cast(v, 32 + 4 * k)
             rs_start(v, f"m3{k}")
 
-    def scatter_rest():
+    def scatter_rest(finish):
         def s1(v):
             for k in (3, 2):
                 rs_arrive(v, f"a3{k}")
@@ -379,44 +406,51 @@
 
         def s6(v):
             rs_arrive(v, "m1", "p1")
-            part[v, 0] = part[v, 0] + rb[v, 61].astype(F32) + rb[v, 62].astype(F32)
+            finish(v, part[v, 0] + rb[v, 61].astype(F32) + rb[v, 62].astype(F32))
 
         for step in (s1, s2, s3, s4, s5, s6):
             units(step)
+
+    def scatter_drain():
         units(lambda v: [scatter_copy(n, v).wait_send() for n in SCATTER])
 
-    def scattered():
-        return jnp.concatenate([part[lax.rem(u + 2 * core, 4), 0] for u in range(4)], axis=0)
-
     def spread(pair, f, product):
-        fy, fz = lax.div(f, 4), lax.rem(f, 4)
         for j in range(2):
-            for ty in range(2):
-                for tx in range(4):
-                    at = place(turn(2 * pair + j), tx, fy * 2 + ty, fz)
-                    row = 128 * j + 64 * ty + 16 * tx
-                    part[2 * pair + j, at] = product[row : row + 16]
-
-    tokens = tok_ref[...].astype(F32)
-    share_stats(0, tokens, small_ref[:, 2176:2304])
+            v = 2 * pair + j
+            for i, at in enumerate(places(unit_strides[v], f)):
+                row = 128 * j + 16 * i
+                part[v, at] = product[row : row + 16]
+
+    for v in range(4):
+        ag[v, 0] = tok_ref[token_unit(v), :]
+    square_sums = square_row(tok_ref[...].astype(F32))
+    blank = jnp.zeros((2, 128), F32)
+    stats[0] = jnp.concatenate(
+        [square_sums, small_ref[17:18], blank, small_ref[0:8], blank, blank], axis=0
+    )
     pl.semaphore_wait(barrier, len(greeted))
+    units(gather_begin)
     for d in range(1, 16):
         stat_copy(0, d).start()
     for copy in remote_copies[:2]:
         copy.start()
-    for d in range(1, 16):
-        stat_copy(0, d).wait_recv()
-    normalize_into_gather(0, tokens, small_ref[:, :512])
+
+    def beside_first(i):
+        if i == 0:
+            spread_roots(0)
+            for copy in out_remote + remote_copies[2:] + down_remote:
+                copy.start()
+        elif i == 4:
+            collect_roots(0)
+
+    gather(beside_first)
     documents = jnp.sum(
-        jnp.where(lax.broadcasted_iota(jnp.int32, (16, 8, 128), 1) == 1, stats[0], 0.0), axis=1
+        jnp.where(lax.broadcasted_iota(jnp.int32, (16, 16, 128), 1) == 1, stats[...], 0.0), axis=1
     )
-    for copy in out_remote + remote_copies[2:] + down_remote:
-        copy.start()
     for copy in local_copies[:2] + table_copies:
         copy.wait()
     for copy in remote_copies[:2]:
         copy.wait_recv()
-    gather()
 
     acckv[...] = jnp.zeros_like(acckv)
 
@@ -425,7 +459,9 @@
         for mine in (True, False):
             cols = feature_columns(f, mine)
             weights = jnp.concatenate([wkv[0, :, cols], wkv[1, :, cols]], axis=0)
-            acckv[...] += dot_nt(weights, gathered(f, mine))
+            block = normalized(f, mine, 4)
+            an[2 * f + (0 if mine else 1)] = block
+            acckv[...] += dot_nt(weights, block)
 
     kv_sum = acckv[...]
     kvall[core, chip] = jnp.concatenate([kv_sum[0:8], kv_sum[16:24], kv_sum[8:16], kv_sum[24:32]], axis=0)
@@ -448,10 +484,9 @@
         for mine in (True, False):
             cols = feature_columns(f, mine)
             weights = jnp.concatenate([wq[0, :, cols], wq[1, :, cols]], axis=0)
-            accq[...] += dot_nt(gathered(f, mine), weights)
-
-    bias_at = pl.ds(pl.multiple_of(1024 + 128 * chip, 128), 128)
-    query = accq[...] + small_ref[:, bias_at]
+            accq[...] += dot_nt(an[2 * f + (0 if mine else 1)], weights)
+
+    query = accq[...] + small_ref[pl.ds(8 + chip, 1), :]
     own_rows = pl.ds(pl.multiple_of(256 * core, 256), 256)
     turned = jnp.concatenate([query[:, 64:], query[:, :64]], axis=1)
     queries = (query * cosq[own_rows, :] + turned * sinq[own_rows, :]).astype(BF)
@@ -493,7 +528,7 @@
     query_position, _, _ = token_parts(lax.broadcasted_iota(jnp.int32, (256, 512), 0), core)
     allowed = (key_position <= query_position) & (key_docs == query_docs)
 
-    value_bias = jnp.transpose(jnp.broadcast_to(small_ref[:, 2048:2176], (128, 128)))
+    value_bias = jnp.transpose(jnp.broadcast_to(small_ref[16:17], (128, 128)))
     value_bias = jnp.concatenate([value_bias] * 2, axis=1)
     remote(kvall.at[1 - core], kvall.at[1 - core], kf_send, kf_recv, partner).wait_recv()
     key_parts, value_parts = [], []
@@ -531,34 +566,44 @@
 
         units(scatter_first, 2 * pair, 2 * pair + 2)
     gather_drain()
-    scatter_rest()
-
-    resid[...] = (tok_ref[...].astype(F32) + scattered()).astype(BF)
-
-    values = resid[...].astype(F32)
-    share_stats(1, values, None)
+
+    def finish_first(v, total):
+        block = (tok_ref[token_unit(v), :].astype(F32) + total).astype(BF)
+        resid[token_unit(v), :] = block
+        ag[v, 0] = block
+        gather_begin(v)
+
+    scatter_rest(finish_first)
+    square_sums = square_row(resid[...].astype(F32))
+    row = lax.broadcasted_iota(jnp.int32, (8, 128), 0)
+    sums[0] = jnp.where(row == 0, square_sums, jnp.zeros((8, 128), F32))
     for d in range(1, 16):
         stat_copy(1, d).start()
+
+    def beside_second(i):
+        if i == 1:
+            spread_roots(1)
+        elif i == 3:
+            scatter_drain()
+        elif i == 4:
+            collect_roots(1)
+
+    gather(beside_second)
     for copy in local_copies[2:]:
         copy.wait()
     for copy in remote_copies[2:]:
         copy.wait_recv()
-    for d in range(1, 16):
-        stat_copy(1, d).wait_recv()
-    normalize_into_gather(1, values, small_ref[:, 512:1024])
-    gather()
 
     accg[...] = jnp.zeros_like(accg)
     accu[...] = jnp.zeros_like(accu)
 
     @pl.loop(0, 8)
     def _(f):
-        for mine in (True, False):
-            cols = feature_columns(f, mine)
-            block = gathered(f, mine)
-            for side in range(2):
-                accg[side] += dot_nt(block, wg[side, :, cols])
-                accu[side] += dot_nt(block, wu[side, :, cols])
+        blocks = [normalized(f, mine, 8) for mine in (True, False)]
+        cols = [feature_columns(f, mine) for mine in (True, False)]
+        for side in range(2):
+            accg[side] += dot_nt(blocks[0], wg[side, :, cols[0]]) + dot_nt(blocks[1], wg[side, :, cols[1]])
+            accu[side] += dot_nt(blocks[0], wu[side, :, cols[0]]) + dot_nt(blocks[1], wu[side, :, cols[1]])
 
     for side in range(2):
         gate = accg[side]
@@ -580,12 +625,18 @@
 
         units(scatter_first, 2 * pair, 2 * pair + 2)
     gather_drain()
-    scatter_rest()
-    out_ref[...] = (resid[...].astype(F32) + scattered()).astype(BF)
-
+
+    def finish_second(v, total):
+        out_ref[token_unit(v), :] = (resid[token_unit(v), :].astype(F32) + total).astype(BF)
+
+    scatter_rest(finish_second)
+    scatter_drain()
     for d in range(1, 16):
         stat_copy(0, d).wait_send()
         stat_copy(1, d).wait_send()
+    for e in range(1, 8):
+        root_copy(0, e).wait_send()
+        root_copy(1, e).wait_send()
     for d in range(1, 8):
         kv_copy(d).wait_send()
     forward.wait_send()
@@ -618,7 +669,7 @@
             attn_gain.astype(F32), ffn_gain.astype(F32), query_bias.astype(F32), value_bias.astype(F32),
             segment_ids.astype(F32), jnp.zeros((96,), F32),
         ]
-    )[None, :]
+    ).reshape(18, 128)
     kv_weight = jnp.concatenate([key_weight, value_weight], axis=0)
     units = gate_weight.shape[0]
     any_spec = pl.BlockSpec(memory_space=pl.ANY)
@@ -643,10 +694,15 @@
             pltpu.VMEM((512, 128), F32),
             pltpu.VMEM((4, 64, ROWS, BLOCK), BF),
             pltpu.VMEM((2, 64, ROWS, BLOCK), BF),
+            pltpu.VMEM((16, 256, BLOCK), BF),
             pltpu.VMEM((4, 64, ROWS, BLOCK), F32),
             pltpu.VMEM((4, 64, ROWS, BLOCK), BF),
             pltpu.VMEM((4, 63, ROWS, BLOCK), BF),
-            pltpu.VMEM((2, 16, 8, 128), F32),
+            pltpu.VMEM((16, 16, 128), F32),
+            pltpu.VMEM((16, 8, 128), F32),
+            pltpu.VMEM((2, 8, 8, 128), F32),
+            pltpu.VMEM((128, 128), F32),
+            pltpu.VMEM((256, 128), F32),
             pltpu.VMEM((2, 8, 32, 256), F32),
             pltpu.VMEM((2, 256, 128), BF),
             pltpu.VMEM((2, 2, 256, units), BF),
@@ -658,7 +714,7 @@
             dma((4, gathers)), dma((4, gathers)),
             dma((2, 4)), dma((2, 4)),
             dma((4, scatters)), dma((4, scatters)),
-            dma((2, 16)), dma((2, 16)),
+            dma((16,)), dma((16,)), dma((16,)), dma((16,)), dma((2, 8)), dma((2, 8)),
             dma((8,)), dma((8,)),
             dma, dma, dma, dma, dma, dma,
             dma((8,)), dma((4,)), dma((4,)),

time: 162 us -> 151 us (0.932)
  Pallas kernels: 155 us -> 144 us
    pallas_call x1, Pallas kernels: 155 us -> 144 us  [shards(): pl.pallas_call(kernel, out_shape=jax.ShapeDtypeStruct((64, BLOCK), BF), i...]
where the time goes in v3:
time: 151 us
  Pallas kernels  144 us (95%)
  local copies, waits for them, and re-layouts  4.87 us (3%)
  other arithmetic  2.33 us (2%)
    pallas_call x1, Pallas kernels, shards(): pl.pallas_call(kernel, out_shape=jax.ShapeDtypeStruct((64, BLOCK), BF), i...  144 us
    concatenate x1, local copies, waits for them, and re-layouts, shards(): jnp.concatenate([attn_gain.astype(F32), ffn_gain.astype(F32), query_bias....  3.39 us

profile of v3, /device:TPU:0, one launch (start us, length us, event | category | flops | bytes accessed | tf_op | source)
XLA Modules:
  0.0 151.0 jit_solution(10115596316903109056)
XLA Ops:
  0.0 0.7 convert_element_type.19
  0.7 3.4 %concatenate.6 = f32[2304]{0:T(1024)} concatenate(bf16[512]{0:T(512)(128)(2,1)} %param.19, bf16[512]{0:T(512)(128)(2,1)} %param.26, bf16[1024]{0:T(1024)(128)(2,1)} %param.21, bf16[128]{0:T(256)(128)(2,1)} %param.24, f32[32]{0:T(128)S(1)} %convert_element_type.19, f32[96]{0:T(128)S(1)} %broadcast_in_dim.3), dimensions={0} | concatenate | bytes 14080 | tf_op jit(solution)/shard_map/concatenate | solution.py:667
  4.1 1.7 %pad_maximum_fusion.wkv_hbm = bf16[16,8192]{1,0:T(8,128)(2,1)} fusion(bf16[8,8192]{1,0:T(8,128)(2,1)} %param.23, bf16[8,8192]{1,0:T(8,128)(2,1)} %param.22), kind=kLoop, calls=%fused_computation | loop fusion | flops 524288 | bytes 524288 | tf_op jit(solution)/shard_map/concatenate | solution.py:673
  5.7 143.7 %layer.1 = bf16[64,512]{1,0:T(8,128)(2,1)} custom-call(bf16[64,512]{1,0:T(8,128)(2,1)} %tok_ref.1, f32[18,128]{1,0:T(8,128)} %bitcast.1, bf16[64,8192]{1,0:T(8,128)(2,1)} %wq_hbm.1, bf16[16,8192]{1,0:T(8,128)(2,1)} %pad_maximum_fusion.wkv_hbm, bf16[64,8192]{1,0:T(8,128)(2,1)} %wo_hbm.1, bf16[231,8192]{1,0:T(8,128)(2,1)} %wg_hbm.1, bf16[231,8192]{1,0:T(8,128)(2,1)} %wu_hbm.1, ...), custom_call_target="tpu_custom_call" | custom-call | tf_op jit(solution)/shard_map/layer/pallas_call | solution.py:679
  149.5 1.5 copy.19
  (1 shorter events, 0.0 us)

commit v4 on v3

--- a/solution.py
+++ b/solution.py
@@ -30,48 +30,32 @@
     return lax.dot_general(left, right, (((1,), (0,)), ((), ())), preferred_element_type=F32)
 
 
-GATHER = {
-    "s1p": (0, 2, 1, 0, 512, 1, 1),
-    "s1m": (0, 1, 1, 0, 512, 1, 3),
-    "f1m": (1, 3, 1, 0, 256, 1, 3),
-    "f1p": (2, 3, 1, 256, 256, 1, 1),
-    "o2p": (0, 8, 1, 0, 512, 2, 1),
-    "o2m": (0, 4, 1, 0, 512, 2, 3),
-    "r2p": (1, 9, 3, 0, 512, 2, 1),
-    "r2m": (1, 5, 3, 0, 512, 2, 3),
-    "f2m": (4, 12, 2, 0, 512, 2, 3),
-    "f2p": (10, 14, 2, 0, 512, 2, 1),
-    "o3p": (0, 32, 1, 0, 512, 3, 1),
-    "o3m": (0, 16, 1, 0, 512, 3, 3),
-    "r3p": (1, 33, 3, 0, 512, 3, 1),
-    "r3m": (1, 17, 3, 0, 512, 3, 3),
-    "f3m0": (16, 48, 4, 0, 512, 3, 3),
-    "f3m1": (20, 52, 4, 0, 512, 3, 3),
-    "f3p2": (40, 56, 4, 0, 512, 3, 1),
-    "f3p3": (44, 60, 4, 0, 512, 3, 1),
-}
-for _k in (1, 2, 3):
-    GATHER[f"g3p{_k}"] = (4 * _k, 32 + 4 * _k, 4, 0, 512, 3, 1)
-    GATHER[f"g3m{_k}"] = (4 * _k, 16 + 4 * _k, 4, 0, 512, 3, 3)
-GATHER_ID = {name: i for i, name in enumerate(GATHER)}
+GATHER = {}
+for _sign, _seen in ((1, 2), (3, 1), (2, 3)):
+    GATHER[f"own1_{_sign}"] = (0, _seen, 1, 1, _sign, 0)
+    GATHER[f"own2_{_sign}"] = (0, 4 * _seen, 1, 2, _sign, 1)
+    GATHER[f"row2_{_sign}"] = (1, 4 * _seen + 1, 3, 2, _sign, 2)
+for _sign, _seen in ((1, 2), (3, 1)):
+    for _k in range(4):
+        GATHER[f"one3_{_k}_{_sign}"] = (4 * _k, 16 * _seen + 4 * _k, 1, 3, _sign, 4 * _seen + _k)
+        GATHER[f"row3_{_k}_{_sign}"] = (4 * _k + 1, 16 * _seen + 4 * _k + 1, 3, 3, _sign, 4 * _seen + _k)
+for _k in range(4):
+    GATHER[f"pass3_{_k}_3"] = (16 + 4 * _k, 48 + 4 * _k, 2, 3, 3, 3)
+    GATHER[f"pass3_{_k}_1"] = (32 + 4 * _k + 2, 48 + 4 * _k + 2, 2, 3, 1, 3)
+ARRIVING = {0: 3, 1: 3, 2: 9, 3: 16, **{i: 4 for i in range(4, 12)}}
 
 SCATTER = {}
-for _i, _k in enumerate((3, 2)):
-    SCATTER[f"a3{_k}"] = (48 + 4 * _k, 4 * _i, 4, 0, 512, 3, 1)
-for _i, _k in enumerate((1, 0)):
-    SCATTER[f"b3{_k}"] = (48 + 4 * _k, 8 + 4 * _i, 4, 0, 512, 3, 3)
+for _k in (3, 2):
+    SCATTER[f"far3_{_k}"] = (48 + 4 * _k, 4 * (3 - _k), 4, 3, 1, _k)
+for _k in (1, 0):
+    SCATTER[f"far3_{_k}"] = (48 + 4 * _k, 8 + 4 * (1 - _k), 4, 3, 3, _k)
 for _k in range(4):
-    SCATTER[f"p3{_k}"] = (16 + 4 * _k, 16 + 4 * _k, 4, 0, 512, 3, 1)
-    SCATTER[f"m3{_k}"] = (32 + 4 * _k, 32 + 4 * _k, 4, 0, 512, 3, 3)
-SCATTER["a2"] = (14, 48, 2, 0, 512, 2, 1)
-SCATTER["b2"] = (12, 50, 2, 0, 512, 2, 3)
-SCATTER["p2"] = (4, 52, 4, 0, 512, 2, 1)
-SCATTER["m2"] = (8, 56, 4, 0, 512, 2, 3)
-SCATTER["a1"] = (3, 60, 1, 0, 256, 1, 1)
-SCATTER["b1"] = (3, 60, 1, 256, 256, 1, 3)
-SCATTER["p1"] = (1, 61, 1, 0, 512, 1, 1)
-SCATTER["m1"] = (2, 62, 1, 0, 512, 1, 3)
-SCATTER_ID = {name: i for i, name in enumerate(SCATTER)}
+    SCATTER[f"up3_{_k}"] = (16 + 4 * _k, 16 + 4 * _k, 4, 3, 1, 4 + _k)
+    SCATTER[f"down3_{_k}"] = (32 + 4 * _k, 32 + 4 * _k, 4, 3, 3, 4 + _k)
+for _k, _sign in ((1, 1), (2, 3), (3, 2)):
+    SCATTER[f"to2_{_k}"] = (4 * _k, 44 + 4 * _k, 4, 2, _sign, 8)
+    SCATTER[f"to1_{_k}"] = (_k, 59 + _k, 1, 1, _sign, 9)
+SUMMED = {**{i: 4 for i in range(4)}, **{i: 8 for i in range(4, 8)}, 8: 12, 9: 3}
 
 
 def one_hot3(value):
@@ -80,11 +64,12 @@
 
 
 def kernel(
-    tok_ref, small_ref, wq_hbm, wkv_hbm, wo_hbm, wg_hbm, wu_hbm, wd_hbm,
+    tok_ref, segment_ref, gain_ref, ffn_gain_ref, query_bias_ref, value_bias_ref,
+    wq_hbm, wk_hbm, wv_hbm, wo_hbm, wg_hbm, wu_hbm, wd_hbm,
     cosk_hbm, sink_hbm, cosq_hbm, sinq_hbm,
     out_ref,
     wq, wkv, wo, wg, wu, wd, cosk, sink, cosq, sinq,
-    ag, xb, an, part, sb, rb, stats, sums, roots, tall, scale, kvall, att, hid, accq, acckv, accg, accu, resid,
+    ag, xb, an, part, sb, rb, stats, sums, roots, tall, scale, bias, kvall, att, hid, accq, acckv, accg, accu, resid,
     ag_send, ag_recv, px_send, px_recv, rs_send, rs_recv, st_send, st_recv, su_send, su_recv, ro_send, ro_recv,
     kv_send, kv_recv, kf_send, kf_recv, at_send, at_recv, hd_send, hd_recv,
     wl_sem, ws_sem, wr_sem, ol_sem, os_sem, or_sem, dl_sem, ds_sem, dr_sem,
@@ -108,7 +93,7 @@
         return device(lax.rem(x + sign * e0, 4), lax.rem(y + sign * e1, 4), lax.rem(z + sign * e2, 4))
 
     neighbours = {
-        (v, level, sign): neighbour(v, level, sign) for v in range(4) for level in (1, 2, 3) for sign in (1, 3)
+        (v, level, sign): neighbour(v, level, sign) for v in range(4) for level in (1, 2, 3) for sign in (1, 2, 3)
     }
 
     def toward(v, level, sign):
@@ -146,23 +131,26 @@
     for target in greeted:
         pl.semaphore_signal(barrier, inc=1, device_id=target, device_id_type=MESH)
 
-    whole = ((wq_hbm, wq), (wkv_hbm, wkv), (wg_hbm, wg), (wu_hbm, wu))
+    whole = (
+        (wq_hbm, wq.at[core]), (wk_hbm, wkv.at[core, 0]), (wv_hbm, wkv.at[core, 1]),
+        (wg_hbm, wg.at[core]), (wu_hbm, wu.at[core]),
+    )
     tables = ((cosk_hbm, cosk), (sink_hbm, sink), (cosq_hbm, cosq), (sinq_hbm, sinq))
     local_copies = [
-        pltpu.make_async_copy(src, dst.at[core], wl_sem.at[i]) for i, (src, dst) in enumerate(whole)
+        pltpu.make_async_copy(src, dst, wl_sem.at[i]) for i, (src, dst) in enumerate(whole)
     ]
     table_copies = [
-        pltpu.make_async_copy(src, dst, wl_sem.at[4 + i]) for i, (src, dst) in enumerate(tables)
+        pltpu.make_async_copy(src, dst, wl_sem.at[5 + i]) for i, (src, dst) in enumerate(tables)
     ]
     remote_copies = [
-        remote(src, dst.at[core], ws_sem.at[i], wr_sem.at[i], partner) for i, (src, dst) in enumerate(whole)
+        remote(src, dst, ws_sem.at[i], wr_sem.at[i], partner) for i, (src, dst) in enumerate(whole)
     ]
     columns = lambda f, side: pl.ds(pl.multiple_of((2 * f + side) * BLOCK, BLOCK), BLOCK)
     out_local = [pltpu.make_async_copy(wo_hbm.at[:, columns(f, core)], wo.at[core, f], ol_sem.at[f]) for f in range(8)]
     down_local = [pltpu.make_async_copy(wd_hbm.at[:, columns(f, core)], wd.at[core, f], dl_sem.at[f]) for f in range(8)]
     out_remote = [remote(wo_hbm.at[:, columns(f, 1 - core)], wo.at[core, f], os_sem.at[f], or_sem.at[f], partner) for f in range(8)]
     down_remote = [remote(wd_hbm.at[:, columns(f, 1 - core)], wd.at[core, f], ds_sem.at[f], dr_sem.at[f], partner) for f in range(8)]
-    for copy in local_copies[:2] + table_copies + out_local + local_copies[2:] + down_local:
+    for copy in local_copies[:3] + table_copies + out_local + local_copies[3:] + down_local:
         copy.start()
 
     def token_unit(v):
@@ -215,17 +203,15 @@
         return (block * jnp.concatenate([factor] * 4, axis=1) * gain).astype(BF)
 
     def gather_copy(name, v):
-        src, dst, count, col, width, level, sign = GATHER[name]
-        i = GATHER_ID[name]
-        if width == 512:
-            a, b = ag.at[v, pl.ds(src, count)], ag.at[v, pl.ds(dst, count)]
-        else:
-            a, b = ag.at[v, src, :, pl.ds(col, width)], ag.at[v, dst, :, pl.ds(col, width)]
-        return remote(a, b, ag_send.at[v, i], ag_recv.at[v, i], toward(v, level, sign))
+        src, dst, count, level, sign, arrival = GATHER[name]
+        return remote(
+            ag.at[v, pl.ds(src, count)], ag.at[v, pl.ds(dst, count)], ag_send.at[v], ag_recv.at[v, arrival],
+            toward(v, level, sign),
+        )
 
     def px_copy(j, k):
         return remote(
-            ag.at[2 + j, pl.ds(16 * k, 16)], xb.at[j, pl.ds(16 * k, 16)], px_send.at[j, k], px_recv.at[j, k], partner
+            ag.at[2 + j, pl.ds(16 * k, 16)], xb.at[j, pl.ds(16 * k, 16)], px_send.at[j], px_recv.at[j], partner
         )
 
     def units(body, first=0, last=4):
@@ -233,75 +219,72 @@
             body(v)
 
     def gather_begin(v):
-        for name in ("s1p", "s1m", "o2p", "o2m", "o3p", "o3m"):
-            gather_copy(name, v).start()
+        for sign in (1, 3, 2):
+            gather_copy(f"own1_{sign}", v).start()
+        for sign in (1, 3):
+            gather_copy(f"one3_0_{sign}", v).start()
+        for sign in (1, 3, 2):
+            gather_copy(f"own2_{sign}", v).start()
 
     def gather(beside):
-        start = lambda v, *names: [gather_copy(n, v).start() for n in names]
-        arrive = lambda v, *names: [gather_copy(n, v).wait_recv() for n in names]
+        def start(v, *names):
+            for n in names:
+                gather_copy(n, v).start()
+
+        def arrive(v, *arrivals):
+            for a in arrivals:
+                blocks = ag.at[v, pl.ds(0, ARRIVING[a])]
+                pltpu.make_async_copy(blocks, blocks, ag_recv.at[v, a]).wait()
 
         def t1(v):
-            arrive(v, "s1m")
-            start(v, "f1m")
-            arrive(v, "s1p")
-            start(v, "f1p")
+            arrive(v, 0)
+            start(v, "row2_1", "row2_3", "row2_2", "row3_0_1", "row3_0_3")
 
         def t2(v):
-            arrive(v, "f1m", "f1p")
-            start(v, "r2p", "r2m", "r3p", "r3m")
+            arrive(v, 1)
+            for k in (1, 2, 3):
+                start(v, f"one3_{k}_1", f"one3_{k}_3")
 
         def t3(v):
-            arrive(v, "o2m", "r2m")
-            start(v, "f2m", "g3p1", "g3m1")
-            arrive(v, "o2p", "r2p")
-            start(v, "f2p", "g3p2", "g3m2")
+            arrive(v, 4, 8)
+            start(v, "pass3_0_3", "pass3_0_1")
 
         def t4(v):
-            arrive(v, "o3m", "r3m")
-            start(v, "f3m0")
-
-        def t5(v):
-            arrive(v, "f2m", "f2p")
-            start(v, "g3p3", "g3m3")
-
-        def t6(v):
-            arrive(v, "g3m1")
-            start(v, "f3m1")
-            arrive(v, "o3p", "r3p", "g3p1", "g3p2")
-            start(v, "f3p2")
-
-        def t7(v):
-            arrive(v, "g3p3")
-            start(v, "f3p3")
-            arrive(v, "g3m2", "g3m3")
-
-        def t8(v):
-            arrive(v, "f3m0", "f3m1", "f3p2", "f3p3")
-
-        for i, step in enumerate((t1, t2, t3, t4, t5)):
+            arrive(v, 2)
+            for k in (1, 2, 3):
+                start(v, f"row3_{k}_1", f"row3_{k}_3")
+
+        def passing(k):
+            def step(v):
+                arrive(v, 4 + k, 8 + k)
+                start(v, f"pass3_{k}_3", f"pass3_{k}_1")
+
+            return step
+
+        for i, step in enumerate((t1, t2, t3, t4)):
             units(step)
             beside(i)
         for j in range(2):
             px_copy(j, 0).start()
-        units(t6)
-        units(t7, 2, 4)
+        for k in (1, 2, 3):
+            units(passing(k))
         for j in range(2):
             px_copy(j, 1).start()
             px_copy(j, 2).start()
-        units(t7, 0, 2)
-        units(t8, 2, 4)
+        beside(4)
         for j in range(2):
+            arrive(2 + j, 3)
             px_copy(j, 3).start()
-        units(t8, 0, 2)
+        units(lambda v: arrive(v, 3), 0, 2)
         for j in range(2):
-            for k in range(4):
-                px_copy(j, k).wait_recv()
+            pltpu.make_async_copy(xb.at[j], xb.at[j], px_recv.at[j]).wait()
 
     def gather_drain():
-        units(lambda v: [gather_copy(n, v).wait_send() for n in GATHER])
+        for v in range(4):
+            blocks = ag.at[v, pl.ds(0, 63)]
+            pltpu.make_async_copy(blocks, blocks, ag_send.at[v]).wait()
         for j in range(2):
-            for k in range(4):
-                px_copy(j, k).wait_send()
+            pltpu.make_async_copy(xb.at[j], xb.at[j], px_send.at[j]).wait()
 
     def gathered(f, mine):
         pieces = []
@@ -314,21 +297,20 @@
         return columns(f, core if mine else 1 - core)
 
     def scatter_copy(name, v):
-        src, dst, count, col, width, level, sign = SCATTER[name]
-        i = SCATTER_ID[name]
-        if width == 512:
-            a, b = sb.at[v, pl.ds(src, count)], rb.at[v, pl.ds(dst, count)]
-        else:
-            a, b = sb.at[v, src, :, pl.ds(col, width)], rb.at[v, dst, :, pl.ds(col, width)]
-        return remote(a, b, rs_send.at[v, i], rs_recv.at[v, i], toward(v, level, sign))
+        src, dst, count, level, sign, arrival = SCATTER[name]
+        return remote(
+            sb.at[v, pl.ds(src, count)], rb.at[v, pl.ds(dst, count)], rs_send.at[v], rs_recv.at[v, arrival],
+            toward(v, level, sign),
+        )
 
     def rs_start(v, *names):
         for n in names:
             scatter_copy(n, v).start()
 
-    def rs_arrive(v, *names):
-        for n in names:
-            scatter_copy(n, v).wait_recv()
+    def rs_arrive(v, *arrivals):
+        for a in arrivals:
+            blocks = rb.at[v, pl.ds(0, SUMMED[a])]
+            pltpu.make_async_copy(blocks, blocks, rs_recv.at[v, a]).wait()
 
     def cast(v, src, count=4):
         sb[v, pl.ds(src, count)] = part[v, pl.ds(src, count)].astype(BF)
@@ -339,80 +321,66 @@
         ).astype(BF)
 
     def scatter_first(v):
-        for k in (3, 2):
+        for k in (3, 1, 2, 0):
             cast(v, 48 + 4 * k)
-            rs_start(v, f"a3{k}")
-        for k in (1, 0):
-            cast(v, 48 + 4 * k)
-            rs_start(v, f"b3{k}")
+            rs_start(v, f"far3_{k}")
         for k in (3, 2):
             cast(v, 32 + 4 * k)
-            rs_start(v, f"m3{k}")
+            rs_start(v, f"down3_{k}")
+        cast(v, 16 + 4 * 1)
+        rs_start(v, "up3_1")
 
     def scatter_rest(finish):
         def s1(v):
             for k in (3, 2):
-                rs_arrive(v, f"a3{k}")
+                rs_arrive(v, k)
                 cast_sum(v, 16 + 4 * k, 4 * (3 - k))
-                rs_start(v, f"p3{k}")
+                rs_start(v, f"up3_{k}")
             for k in (1, 0):
-                cast(v, 16 + 4 * k)
-                rs_start(v, f"p3{k}")
-                rs_arrive(v, f"b3{k}")
+                rs_arrive(v, k)
                 cast_sum(v, 32 + 4 * k, 8 + 4 * (1 - k))
-                rs_start(v, f"m3{k}")
+                rs_start(v, f"down3_{k}")
+            cast(v, 16)
+            rs_start(v, "up3_0")
 
         def total3(v, k):
-            rs_arrive(v, f"m3{k}", f"p3{k}")
+            rs_arrive(v, 4 + k)
             return (
                 part[v, pl.ds(4 * k, 4)]
                 + rb[v, pl.ds(16 + 4 * k, 4)].astype(F32)
                 + rb[v, pl.ds(32 + 4 * k, 4)].astype(F32)
             )
 
-        def s2(v):
-            sb[v, pl.ds(12, 4)] = total3(v, 3).astype(BF)
-            rs_start(v, "a2", "b2")
+        def s2(k):
+            def step(v):
+                sb[v, pl.ds(4 * k, 4)] = total3(v, k).astype(BF)
+                rs_start(v, f"to2_{k}")
+
+            return step
 
         def s3(v):
-            total = total3(v, 2)
-            rs_arrive(v, "b2")
-            sb[v, pl.ds(8, 2)] = (total[:2] + rb[v, pl.ds(50, 2)].astype(F32)).astype(BF)
-            sb[v, pl.ds(10, 2)] = total[2:].astype(BF)
-            rs_start(v, "m2")
-            total = total3(v, 1)
-            rs_arrive(v, "a2")
-            sb[v, pl.ds(6, 2)] = (total[2:] + rb[v, pl.ds(48, 2)].astype(F32)).astype(BF)
-            sb[v, pl.ds(4, 2)] = total[:2].astype(BF)
-            rs_start(v, "p2")
+            total = total3(v, 0)
+            rs_arrive(v, 8)
+            for place_at in (48, 52, 56):
+                total = total + rb[v, pl.ds(place_at, 4)].astype(F32)
+            part[v, 0] = total[0]
+            sb[v, 1:4] = total[1:].astype(BF)
+            rs_start(v, "to1_1", "to1_2", "to1_3")
 
         def s4(v):
-            total = total3(v, 0)
-            rs_arrive(v, "m2", "p2")
-            total = total + rb[v, pl.ds(52, 4)].astype(F32) + rb[v, pl.ds(56, 4)].astype(F32)
-            part[v, pl.ds(0, 4)] = total
-            sb[v, 3] = total[3].astype(BF)
-            rs_start(v, "a1", "b1")
-
-        def s5(v):
-            sb[v, 1, :, 256:] = part[v, 1, :, 256:].astype(BF)
-            rs_arrive(v, "a1")
-            sb[v, 1, :, :256] = (part[v, 1, :, :256] + rb[v, 60, :, :256].astype(F32)).astype(BF)
-            rs_start(v, "p1")
-            sb[v, 2, :, :256] = part[v, 2, :, :256].astype(BF)
-            rs_arrive(v, "b1")
-            sb[v, 2, :, 256:] = (part[v, 2, :, 256:] + rb[v, 60, :, 256:].astype(F32)).astype(BF)
-            rs_start(v, "m1")
-
-        def s6(v):
-            rs_arrive(v, "m1", "p1")
-            finish(v, part[v, 0] + rb[v, 61].astype(F32) + rb[v, 62].astype(F32))
-
-        for step in (s1, s2, s3, s4, s5, s6):
+            rs_arrive(v, 9)
+            total = part[v, 0]
+            for place_at in (60, 61, 62):
+                total = total + rb[v, place_at].astype(F32)
+            finish(v, total)
+
+        for step in (s1, s2(3), s2(2), s2(1), s3, s4):
             units(step)
 
     def scatter_drain():
-        units(lambda v: [scatter_copy(n, v).wait_send() for n in SCATTER])
+        for v in range(4):
+            blocks = sb.at[v, pl.ds(0, 63)]
+            pltpu.make_async_copy(blocks, blocks, rs_send.at[v]).wait()
 
     def spread(pair, f, product):
         for j in range(2):
@@ -424,21 +392,24 @@
     for v in range(4):
         ag[v, 0] = tok_ref[token_unit(v), :]
     square_sums = square_row(tok_ref[...].astype(F32))
-    blank = jnp.zeros((2, 128), F32)
-    stats[0] = jnp.concatenate(
-        [square_sums, small_ref[17:18], blank, small_ref[0:8], blank, blank], axis=0
-    )
+    stats[0] = jnp.zeros((16, 128), F32)
+    stats[0, 0:1] = square_sums
+    stats[0, 1:2, 0:32] = segment_ref[...].astype(F32).reshape(1, 32)
+    stats[0, 4:8] = gain_ref[...].astype(F32).reshape(4, 128)
+    stats[0, 8:12] = ffn_gain_ref[...].astype(F32).reshape(4, 128)
+    bias[0:8] = query_bias_ref[...].astype(F32).reshape(8, 128)
+    bias[8:9] = value_bias_ref[...].astype(F32).reshape(1, 128)
     pl.semaphore_wait(barrier, len(greeted))
     units(gather_begin)
     for d in range(1, 16):
         stat_copy(0, d).start()
-    for copy in remote_copies[:2]:
+    for copy in remote_copies[:3]:
         copy.start()
 
     def beside_first(i):
         if i == 0:
             spread_roots(0)
-            for copy in out_remote + remote_copies[2:] + down_remote:
+            for copy in out_remote + remote_copies[3:] + down_remote:
                 copy.start()
         elif i == 4:
             collect_roots(0)
@@ -447,9 +418,9 @@
     documents = jnp.sum(
         jnp.where(lax.broadcasted_iota(jnp.int32, (16, 16, 128), 1) == 1, stats[...], 0.0), axis=1
     )
-    for copy in local_copies[:2] + table_copies:
+    for copy in local_copies[:3] + table_copies:
         copy.wait()
-    for copy in remote_copies[:2]:
+    for copy in remote_copies[:3]:
         copy.wait_recv()
 
     acckv[...] = jnp.zeros_like(acckv)
@@ -458,13 +429,13 @@
     def _(f):
         for mine in (True, False):
             cols = feature_columns(f, mine)
-            weights = jnp.concatenate([wkv[0, :, cols], wkv[1, :, cols]], axis=0)
+            weights = [wkv[side, kind, :, cols].astype(F32) for kind in range(2) for side in range(2)]
+            weights = jnp.concatenate(weights, axis=0).astype(BF)
             block = normalized(f, mine, 4)
             an[2 * f + (0 if mine else 1)] = block
             acckv[...] += dot_nt(weights, block)
 
-    kv_sum = acckv[...]
-    kvall[core, chip] = jnp.concatenate([kv_sum[0:8], kv_sum[16:24], kv_sum[8:16], kv_sum[24:32]], axis=0)
+    kvall[core, chip] = acckv[...]
 
     def kv_copy(d):
         there = lax.rem(gy + 2 * d, 16)
@@ -486,7 +457,7 @@
             weights = jnp.concatenate([wq[0, :, cols], wq[1, :, cols]], axis=0)
             accq[...] += dot_nt(an[2 * f + (0 if mine else 1)], weights)
 
-    query = accq[...] + small_ref[pl.ds(8 + chip, 1), :]
+    query = accq[...] + bias[pl.ds(chip, 1), :]
     own_rows = pl.ds(pl.multiple_of(256 * core, 256), 256)
     turned = jnp.concatenate([query[:, 64:], query[:, :64]], axis=1)
     queries = (query * cosq[own_rows, :] + turned * sinq[own_rows, :]).astype(BF)
@@ -528,7 +499,7 @@
     query_position, _, _ = token_parts(lax.broadcasted_iota(jnp.int32, (256, 512), 0), core)
     allowed = (key_position <= query_position) & (key_docs == query_docs)
 
-    value_bias = jnp.transpose(jnp.broadcast_to(small_ref[16:17], (128, 128)))
+    value_bias = jnp.transpose(jnp.broadcast_to(bias[8:9], (128, 128)))
     value_bias = jnp.concatenate([value_bias] * 2, axis=1)
     remote(kvall.at[1 - core], kvall.at[1 - core], kf_send, kf_recv, partner).wait_recv()
     key_parts, value_parts = [], []
@@ -589,9 +560,9 @@
             collect_roots(1)
 
     gather(beside_second)
-    for copy in local_copies[2:]:
+    for copy in local_copies[3:]:
         copy.wait()
-    for copy in remote_copies[2:]:
+    for copy in remote_copies[3:]:
         copy.wait_recv()
 
     accg[...] = jnp.zeros_like(accg)
@@ -664,26 +635,18 @@
     tokens, segment_ids, attn_gain, query_weight, query_bias, key_weight, value_weight, value_bias,
     out_weight, ffn_gain, gate_weight, up_weight, down_weight,
 ):
-    small = jnp.concatenate(
-        [
-            attn_gain.astype(F32), ffn_gain.astype(F32), query_bias.astype(F32), value_bias.astype(F32),
-            segment_ids.astype(F32), jnp.zeros((96,), F32),
-        ]
-    ).reshape(18, 128)
-    kv_weight = jnp.concatenate([key_weight, value_weight], axis=0)
     units = gate_weight.shape[0]
     any_spec = pl.BlockSpec(memory_space=pl.ANY)
     vmem_spec = pl.BlockSpec(memory_space=pltpu.VMEM)
     dma = pltpu.SemaphoreType.DMA
-    gathers, scatters = len(GATHER), len(SCATTER)
     return pl.pallas_call(
         kernel,
         out_shape=jax.ShapeDtypeStruct((64, BLOCK), BF),
-        in_specs=[vmem_spec] * 2 + [any_spec] * 10,
+        in_specs=[vmem_spec] * 6 + [any_spec] * 11,
         out_specs=vmem_spec,
         scratch_shapes=[
             pltpu.VMEM((2, 64, MODEL), BF),
-            pltpu.VMEM((2, 16, MODEL), BF),
+            pltpu.VMEM((2, 2, 8, MODEL), BF),
             pltpu.VMEM((2, 8, 64, BLOCK), BF),
             pltpu.VMEM((2, units, MODEL), BF),
             pltpu.VMEM((2, units, MODEL), BF),
@@ -703,6 +666,7 @@
             pltpu.VMEM((2, 8, 8, 128), F32),
             pltpu.VMEM((128, 128), F32),
             pltpu.VMEM((256, 128), F32),
+            pltpu.VMEM((16, 128), F32),
             pltpu.VMEM((2, 8, 32, 256), F32),
             pltpu.VMEM((2, 256, 128), BF),
             pltpu.VMEM((2, 2, 256, units), BF),
@@ -711,13 +675,13 @@
             pltpu.VMEM((2, 256, units), F32),
             pltpu.VMEM((2, 256, units), F32),
             pltpu.VMEM((64, BLOCK), BF),
-            dma((4, gathers)), dma((4, gathers)),
-            dma((2, 4)), dma((2, 4)),
-            dma((4, scatters)), dma((4, scatters)),
+            dma((4,)), dma((4, 12)),
+            dma((2,)), dma((2,)),
+            dma((4,)), dma((4, 10)),
             dma((16,)), dma((16,)), dma((16,)), dma((16,)), dma((2, 8)), dma((2, 8)),
             dma((8,)), dma((8,)),
             dma, dma, dma, dma, dma, dma,
-            dma((8,)), dma((4,)), dma((4,)),
+            dma((9,)), dma((5,)), dma((5,)),
             dma((8,)), dma((8,)), dma((8,)),
             dma((8,)), dma((8,)), dma((8,)),
         ],
@@ -726,7 +690,8 @@
         ),
         name="layer",
     )(
-        tokens, small, query_weight, kv_weight, out_weight, gate_weight, up_weight, down_weight, *rotary_tables()
+        tokens, segment_ids, attn_gain, ffn_gain, query_bias, value_bias, query_weight, key_weight, value_weight,
+        out_weight, gate_weight, up_weight, down_weight, *rotary_tables(),
     )
 
 

time: 151 us -> 131 us (0.87)
  Pallas kernels: 144 us -> 129 us
  local copies, waits for them, and re-layouts: 4.87 us -> 1.47 us
  other arithmetic: 2.33 us -> 0 us
    pallas_call x1, Pallas kernels: 144 us -> 129 us  [shards(): pl.pallas_call(kernel, out_shape=jax.ShapeDtypeStruct((64, BLOCK), BF), i...]
    concatenate x1 -> x0, local copies, waits for them, and re-layouts: 3.39 us -> none  [shards(): jnp.concatenate([attn_gain.astype(F32), ffn_gain.astype(F32), query_bias....]
    concatenate x1 -> x0, other arithmetic: 1.68 us -> none  [shards(): kv_weight = jnp.concatenate([key_weight, value_weight], axis=0)]
where the time goes in v4:
time: 131 us
  Pallas kernels  129 us (98%)
  local copies, waits for them, and re-layouts  1.47 us (1%)
    pallas_call x1, Pallas kernels, shards(): pl.pallas_call(kernel, out_shape=jax.ShapeDtypeStruct((64, BLOCK), BF), i...  129 us

profile of v4, /device:TPU:0, one launch (start us, length us, event | category | flops | bytes accessed | tf_op | source)
XLA Modules:
  0.0 130.9 jit_solution(11792887647555379011)
XLA Ops:
  0.0 129.4 %layer.1 = bf16[64,512]{1,0:T(8,128)(2,1)} custom-call(bf16[64,512]{1,0:T(8,128)(2,1)} %tok_ref.1, s32[32]{0:T(128)} %segment_ref.1, bf16[512]{0:T(512)(128)(2,1)} %gain_ref.1, bf16[512]{0:T(512)(128)(2,1)} %ffn_gain_ref.1, bf16[1024]{0:T(1024)(128)(2,1)} %query_bias_ref.1, bf16[128]{0:T(256)(128)(2,1)} %value_bias_ref.1, bf16[64,8192]{1,0:T(8,128)(2,1)} %wq_hbm.1, ...), custom_call_target="tpu_custom_call" | custom-call | tf_op jit(solution)/shard_map/layer/pallas_call | solution.py:642
  129.4 1.5 %copy.19 = bf16[64,512]{1,0:T(8,128)(2,1)} copy(bf16[64,512]{1,0:T(8,128)(2,1)} %layer.1) | data formatting | bytes 131072

commit v5 on v4

--- a/solution.py
+++ b/solution.py
@@ -84,12 +84,13 @@
     def device(x, y, z):
         return (lax.rem(y, 2) * 4 + x, lax.div(y, 2) * 8 + z * 2 + core)
 
-    def turn(v):
-        group, item = lax.div(v, 2), lax.rem(v, 2)
-        return (1 - group) * core * (1 + item) + group * (1 + item - core)
+    own_orders = [(0, 1), (2 * core, 1), (1 + core, 0), (1, core)]
+    other_orders = [(2 - core, 0), (1, 1 - core)]
 
     def neighbour(v, level, sign):
-        e0, e1, e2 = one_hot3(lax.rem(turn(v) + 3 - level, 3))
+        bulk, choice = own_orders[v]
+        step = {3: 0, 2: 1 + choice, 1: 2 - choice}[level]
+        e0, e1, e2 = one_hot3(lax.rem(jnp.int32(bulk + step), 3))
         return device(lax.rem(x + sign * e0, 4), lax.rem(y + sign * e1, 4), lax.rem(z + sign * e2, 4))
 
     neighbours = {
@@ -103,13 +104,17 @@
         d = lax.rem(position - mine + 4, 4)
         return d + lax.div(d, 2) - 2 * lax.div(d, 3)
 
-    def strides(rotation):
-        e0, e1, e2 = one_hot3(rotation)
-        return 16 * e0 + e1 + 4 * e2, 4 * e0 + 16 * e1 + e2, e0 + 4 * e1 + 16 * e2
+    def strides(order):
+        bulk, choice = order
+        result = []
+        for axis in range(3):
+            e0, e1, e2 = one_hot3(lax.rem(jnp.int32(axis + 3 - bulk), 3))
+            result.append(16 * e0 + (4 - 3 * choice) * e1 + (1 + 3 * choice) * e2)
+        return result
 
     x_slots = [slot(position, x) for position in range(4)]
-    unit_strides = [strides(turn(v)) for v in range(4)]
-    other_strides = [strides(j + core) for j in range(2)]
+    unit_strides = [strides(order) for order in own_orders]
+    other_strides = [strides(order) for order in other_orders]
 
     def places(stride, f):
         fy, fz = lax.div(f, 4), lax.rem(f, 4)
@@ -145,11 +150,14 @@
     remote_copies = [
         remote(src, dst, ws_sem.at[i], wr_sem.at[i], partner) for i, (src, dst) in enumerate(whole)
     ]
+    def wait_bytes(ref, semaphore):
+        pltpu.make_async_copy(ref, ref, semaphore).wait()
+
     columns = lambda f, side: pl.ds(pl.multiple_of((2 * f + side) * BLOCK, BLOCK), BLOCK)
-    out_local = [pltpu.make_async_copy(wo_hbm.at[:, columns(f, core)], wo.at[core, f], ol_sem.at[f]) for f in range(8)]
-    down_local = [pltpu.make_async_copy(wd_hbm.at[:, columns(f, core)], wd.at[core, f], dl_sem.at[f]) for f in range(8)]
-    out_remote = [remote(wo_hbm.at[:, columns(f, 1 - core)], wo.at[core, f], os_sem.at[f], or_sem.at[f], partner) for f in range(8)]
-    down_remote = [remote(wd_hbm.at[:, columns(f, 1 - core)], wd.at[core, f], ds_sem.at[f], dr_sem.at[f], partner) for f in range(8)]
+    out_local = [pltpu.make_async_copy(wo_hbm.at[:, columns(f, core)], wo.at[core, f], ol_sem) for f in range(8)]
+    down_local = [pltpu.make_async_copy(wd_hbm.at[:, columns(f, core)], wd.at[core, f], dl_sem) for f in range(8)]
+    out_remote = [remote(wo_hbm.at[:, columns(f, 1 - core)], wo.at[core, f], os_sem, or_sem, partner) for f in range(8)]
+    down_remote = [remote(wd_hbm.at[:, columns(f, 1 - core)], wd.at[core, f], ds_sem, dr_sem, partner) for f in range(8)]
     for copy in local_copies[:3] + table_copies + out_local + local_copies[3:] + down_local:
         copy.start()
 
@@ -165,17 +173,16 @@
     def stat_copy(phase, d):
         there = (gx, lax.rem(gy + d, 16))
         if phase == 0:
-            return remote(stats.at[0], stats.at[d], st_send.at[d], st_recv.at[d], there)
-        return remote(sums.at[0], sums.at[d], su_send.at[d], su_recv.at[d], there)
+            return remote(stats.at[0], stats.at[d], st_send, st_recv, there)
+        return remote(sums.at[0], sums.at[d], su_send, su_recv, there)
 
     def root_copy(phase, e):
         return remote(
-            roots.at[phase, 0], roots.at[phase, e], ro_send.at[phase, e], ro_recv.at[phase, e], (lax.rem(gx + e, 8), gy)
+            roots.at[phase, 0], roots.at[phase, e], ro_send.at[phase], ro_recv.at[phase], (lax.rem(gx + e, 8), gy)
         )
 
     def spread_roots(phase):
-        for d in range(1, 16):
-            stat_copy(phase, d).wait_recv()
+        wait_bytes(*((stats.at[pl.ds(1, 15)], st_recv) if phase == 0 else (sums.at[pl.ds(1, 15)], su_recv)))
         summed = jnp.sum(stats[:, :8] if phase == 0 else sums[...], axis=0)
         inverse = lax.rsqrt(summed / MODEL + EPSILON)
         roots[phase, 0] = inverse
@@ -183,8 +190,7 @@
             root_copy(phase, e).start()
 
     def collect_roots(phase):
-        for e in range(1, 8):
-            root_copy(phase, e).wait_recv()
+        wait_bytes(roots.at[phase, pl.ds(1, 7)], ro_recv.at[phase])
         factors = jnp.concatenate([roots[phase, e, :1] for e in range(8)], axis=0)
         tall[...] = jnp.transpose(jnp.concatenate([factors] * 16, axis=0))
         lane = lax.broadcasted_iota(jnp.int32, (16, 128), 1)
@@ -214,8 +220,10 @@
             ag.at[2 + j, pl.ds(16 * k, 16)], xb.at[j, pl.ds(16 * k, 16)], px_send.at[j], px_recv.at[j], partner
         )
 
-    def units(body, first=0, last=4):
-        for v in range(first, last):
+    wave_a, wave_b, in_order = (0, 2), (1, 3), (0, 2, 1, 3)
+
+    def units(body, which=in_order):
+        for v in which:
             body(v)
 
     def gather_begin(v):
@@ -226,58 +234,52 @@
         for sign in (1, 3, 2):
             gather_copy(f"own2_{sign}", v).start()
 
-    def gather(beside):
-        def start(v, *names):
-            for n in names:
-                gather_copy(n, v).start()
-
-        def arrive(v, *arrivals):
-            for a in arrivals:
-                blocks = ag.at[v, pl.ds(0, ARRIVING[a])]
-                pltpu.make_async_copy(blocks, blocks, ag_recv.at[v, a]).wait()
-
-        def t1(v):
-            arrive(v, 0)
-            start(v, "row2_1", "row2_3", "row2_2", "row3_0_1", "row3_0_3")
-
-        def t2(v):
-            arrive(v, 1)
-            for k in (1, 2, 3):
-                start(v, f"one3_{k}_1", f"one3_{k}_3")
-
-        def t3(v):
-            arrive(v, 4, 8)
-            start(v, "pass3_0_3", "pass3_0_1")
-
-        def t4(v):
-            arrive(v, 2)
-            for k in (1, 2, 3):
-                start(v, f"row3_{k}_1", f"row3_{k}_3")
-
-        def passing(k):
-            def step(v):
-                arrive(v, 4 + k, 8 + k)
-                start(v, f"pass3_{k}_3", f"pass3_{k}_1")
-
-            return step
-
-        for i, step in enumerate((t1, t2, t3, t4)):
-            units(step)
-            beside(i)
+    def gather_start(v, *names):
+        for n in names:
+            gather_copy(n, v).start()
+
+    def gather_arrive(v, *arrivals):
+        for a in arrivals:
+            wait_bytes(ag.at[v, pl.ds(0, ARRIVING[a])], ag_recv.at[v, a])
+
+    def t1(v):
+        gather_arrive(v, 0)
+        gather_start(v, "row2_1", "row2_3", "row2_2", "row3_0_1", "row3_0_3")
+
+    def t2(v):
+        gather_arrive(v, 1)
+        for k in (1, 2, 3):
+            gather_start(v, f"one3_{k}_1", f"one3_{k}_3")
+
+    def t3(v):
+        gather_arrive(v, 4, 8)
+        gather_start(v, "pass3_0_3", "pass3_0_1")
+
+    def t4(v):
+        gather_arrive(v, 2)
+        for k in (1, 2, 3):
+            gather_start(v, f"row3_{k}_1", f"row3_{k}_3")
+        if v >= 2:
+            px_copy(v - 2, 0).start()
+
+    def passing(v):
+        for k in (1, 2, 3):
+            gather_arrive(v, 4 + k, 8 + k)
+            gather_start(v, f"pass3_{k}_3", f"pass3_{k}_1")
+        if v >= 2:
+            px_copy(v - 2, 1).start()
+            px_copy(v - 2, 2).start()
+
+    def t5(v):
+        gather_arrive(v, 3)
+        if v >= 2:
+            px_copy(v - 2, 3).start()
+
+    def gather_end():
+        for v in (2, 3, 0, 1):
+            t5(v)
         for j in range(2):
-            px_copy(j, 0).start()
-        for k in (1, 2, 3):
-            units(passing(k))
-        for j in range(2):
-            px_copy(j, 1).start()
-            px_copy(j, 2).start()
-        beside(4)
-        for j in range(2):
-            arrive(2 + j, 3)
-            px_copy(j, 3).start()
-        units(lambda v: arrive(v, 3), 0, 2)
-        for j in range(2):
-            pltpu.make_async_copy(xb.at[j], xb.at[j], px_recv.at[j]).wait()
+            wait_bytes(xb.at[j], px_recv.at[j])
 
     def gather_drain():
         for v in range(4):
@@ -320,74 +322,75 @@
             part[v, pl.ds(src, count)] + rb[v, pl.ds(place_at, count)].astype(F32)
         ).astype(BF)
 
-    def scatter_first(v):
+    def scatter_far(v):
         for k in (3, 1, 2, 0):
             cast(v, 48 + 4 * k)
             rs_start(v, f"far3_{k}")
+
+    def scatter_near(v):
         for k in (3, 2):
             cast(v, 32 + 4 * k)
             rs_start(v, f"down3_{k}")
         cast(v, 16 + 4 * 1)
         rs_start(v, "up3_1")
 
-    def scatter_rest(finish):
-        def s1(v):
-            for k in (3, 2):
-                rs_arrive(v, k)
-                cast_sum(v, 16 + 4 * k, 4 * (3 - k))
-                rs_start(v, f"up3_{k}")
-            for k in (1, 0):
-                rs_arrive(v, k)
-                cast_sum(v, 32 + 4 * k, 8 + 4 * (1 - k))
-                rs_start(v, f"down3_{k}")
-            cast(v, 16)
-            rs_start(v, "up3_0")
-
-        def total3(v, k):
-            rs_arrive(v, 4 + k)
-            return (
-                part[v, pl.ds(4 * k, 4)]
-                + rb[v, pl.ds(16 + 4 * k, 4)].astype(F32)
-                + rb[v, pl.ds(32 + 4 * k, 4)].astype(F32)
-            )
-
-        def s2(k):
-            def step(v):
-                sb[v, pl.ds(4 * k, 4)] = total3(v, k).astype(BF)
-                rs_start(v, f"to2_{k}")
-
-            return step
-
-        def s3(v):
-            total = total3(v, 0)
-            rs_arrive(v, 8)
-            for place_at in (48, 52, 56):
-                total = total + rb[v, pl.ds(place_at, 4)].astype(F32)
-            part[v, 0] = total[0]
-            sb[v, 1:4] = total[1:].astype(BF)
-            rs_start(v, "to1_1", "to1_2", "to1_3")
-
-        def s4(v):
-            rs_arrive(v, 9)
-            total = part[v, 0]
-            for place_at in (60, 61, 62):
-                total = total + rb[v, place_at].astype(F32)
-            finish(v, total)
-
-        for step in (s1, s2(3), s2(2), s2(1), s3, s4):
-            units(step)
+    def s1(v):
+        for k in (3, 2):
+            rs_arrive(v, k)
+            cast_sum(v, 16 + 4 * k, 4 * (3 - k))
+            rs_start(v, f"up3_{k}")
+        for k in (1, 0):
+            rs_arrive(v, k)
+            cast_sum(v, 32 + 4 * k, 8 + 4 * (1 - k))
+            rs_start(v, f"down3_{k}")
+        cast(v, 16)
+        rs_start(v, "up3_0")
+
+    def total3(v, k):
+        rs_arrive(v, 4 + k)
+        return (
+            part[v, pl.ds(4 * k, 4)]
+            + rb[v, pl.ds(16 + 4 * k, 4)].astype(F32)
+            + rb[v, pl.ds(32 + 4 * k, 4)].astype(F32)
+        )
+
+    def s2(k):
+        def step(v):
+            sb[v, pl.ds(4 * k, 4)] = total3(v, k).astype(BF)
+            rs_start(v, f"to2_{k}")
+
+        return step
+
+    def s3(v):
+        total = total3(v, 0)
+        rs_arrive(v, 8)
+        for place_at in (48, 52, 56):
+            total = total + rb[v, pl.ds(place_at, 4)].astype(F32)
+        part[v, 0] = total[0]
+        sb[v, 1:4] = total[1:].astype(BF)
+        rs_start(v, "to1_1", "to1_2", "to1_3")
+
+    def final_sum(v):
+        rs_arrive(v, 9)
+        total = part[v, 0]
+        for place_at in (60, 61, 62):
+            total = total + rb[v, place_at].astype(F32)
+        return total
 
     def scatter_drain():
         for v in range(4):
             blocks = sb.at[v, pl.ds(0, 63)]
             pltpu.make_async_copy(blocks, blocks, rs_send.at[v]).wait()
 
-    def spread(pair, f, product):
-        for j in range(2):
-            v = 2 * pair + j
+    def spread(wave, f, product):
+        for j, v in enumerate((wave, 2 + wave)):
             for i, at in enumerate(places(unit_strides[v], f)):
                 row = 128 * j + 16 * i
                 part[v, at] = product[row : row + 16]
+
+    def wave_rows(ref, wave):
+        rows = pl.ds(128 * wave, 128)
+        return jnp.concatenate([ref[0, rows], ref[1, rows]], axis=0)
 
     for v in range(4):
         ag[v, 0] = tok_ref[token_unit(v), :]
@@ -406,15 +409,16 @@
     for copy in remote_copies[:3]:
         copy.start()
 
-    def beside_first(i):
-        if i == 0:
-            spread_roots(0)
-            for copy in out_remote + remote_copies[3:] + down_remote:
-                copy.start()
-        elif i == 4:
-            collect_roots(0)
-
-    gather(beside_first)
+    units(t1)
+    spread_roots(0)
+    for copy in out_remote + remote_copies[3:] + down_remote:
+        copy.start()
+    units(t2)
+    units(t3)
+    units(t4)
+    units(passing)
+    collect_roots(0)
+    gather_end()
     documents = jnp.sum(
         jnp.where(lax.broadcasted_iota(jnp.int32, (16, 16, 128), 1) == 1, stats[...], 0.0), axis=1
     )
@@ -425,7 +429,7 @@
 
     acckv[...] = jnp.zeros_like(acckv)
 
-    @pl.loop(0, 8)
+    @pl.loop(0, 8, unroll=2)
     def _(f):
         for mine in (True, False):
             cols = feature_columns(f, mine)
@@ -439,18 +443,14 @@
 
     def kv_copy(d):
         there = lax.rem(gy + 2 * d, 16)
-        return remote(kvall.at[core, chip], kvall.at[core, chip], kv_send.at[d], kv_recv.at[d], (gx, there))
-
-    def kv_arrival(d):
-        source = lax.rem(chip + 8 - d, 8)
-        return remote(kvall.at[core, source], kvall.at[core, source], kv_send.at[d], kv_recv.at[d], partner)
+        return remote(kvall.at[core, chip], kvall.at[core, chip], kv_send, kv_recv, (gx, there))
 
     for d in range(1, 8):
         kv_copy(d).start()
 
     accq[...] = jnp.zeros_like(accq)
 
-    @pl.loop(0, 8)
+    @pl.loop(0, 8, unroll=2)
     def _(f):
         for mine in (True, False):
             cols = feature_columns(f, mine)
@@ -462,8 +462,7 @@
     turned = jnp.concatenate([query[:, 64:], query[:, :64]], axis=1)
     queries = (query * cosq[own_rows, :] + turned * sinq[own_rows, :]).astype(BF)
 
-    for d in range(1, 8):
-        kv_arrival(d).wait_recv()
+    wait_bytes(kvall.at[core, pl.ds(0, 7)], kv_recv)
     forward = remote(kvall.at[core], kvall.at[core], kf_send, kf_recv, partner)
     forward.start()
 
@@ -522,44 +521,58 @@
     send_att = remote(att.at[0], att.at[1], at_send, at_recv, partner)
     send_att.start()
 
-    for copy in out_local:
-        copy.wait()
-    for copy in out_remote:
-        copy.wait_recv()
-    for pair in range(2):
-        if pair == 1:
-            send_att.wait_recv()
-
-        @pl.loop(0, 8)
+    wait_bytes(wo.at[core], ol_sem)
+    wait_bytes(wo.at[1 - core], or_sem)
+    send_att.wait_recv()
+
+    def project_out(wave):
+        @pl.loop(0, 8, unroll=2)
         def _(f):
             weights = jnp.concatenate([wo[0, f], wo[1, f]], axis=0)
-            spread(pair, f, dot_nn(att[pair], weights))
-
-        units(scatter_first, 2 * pair, 2 * pair + 2)
-    gather_drain()
-
-    def finish_first(v, total):
-        block = (tok_ref[token_unit(v), :].astype(F32) + total).astype(BF)
+            spread(wave, f, dot_nn(wave_rows(att, wave), weights))
+
+    def finish_first(v):
+        block = (tok_ref[token_unit(v), :].astype(F32) + final_sum(v)).astype(BF)
         resid[token_unit(v), :] = block
         ag[v, 0] = block
         gather_begin(v)
 
-    scatter_rest(finish_first)
+    project_out(0)
+    units(scatter_far, wave_a)
+    units(scatter_near, wave_a)
+    project_out(1)
+    units(scatter_far, wave_b)
+    units(s1, wave_a)
+    units(scatter_near, wave_b)
+    gather_drain()
+    for k in (3, 2, 1):
+        units(s2(k), wave_a)
+    units(s1, wave_b)
+    units(s3, wave_a)
+    for k in (3, 2, 1):
+        units(s2(k), wave_b)
+    units(finish_first, wave_a)
+    units(s3, wave_b)
+    units(t1, wave_a)
+    units(t2, wave_a)
+    units(finish_first, wave_b)
     square_sums = square_row(resid[...].astype(F32))
     row = lax.broadcasted_iota(jnp.int32, (8, 128), 0)
     sums[0] = jnp.where(row == 0, square_sums, jnp.zeros((8, 128), F32))
     for d in range(1, 16):
         stat_copy(1, d).start()
-
-    def beside_second(i):
-        if i == 1:
-            spread_roots(1)
-        elif i == 3:
-            scatter_drain()
-        elif i == 4:
-            collect_roots(1)
-
-    gather(beside_second)
+    units(t3, wave_a)
+    units(t4, wave_a)
+    units(t1, wave_b)
+    units(t2, wave_b)
+    spread_roots(1)
+    units(t3, wave_b)
+    scatter_drain()
+    units(passing, wave_a)
+    units(t4, wave_b)
+    collect_roots(1)
+    units(passing, wave_b)
+    gather_end()
     for copy in local_copies[3:]:
         copy.wait()
     for copy in remote_copies[3:]:
@@ -568,7 +581,7 @@
     accg[...] = jnp.zeros_like(accg)
     accu[...] = jnp.zeros_like(accu)
 
-    @pl.loop(0, 8)
+    @pl.loop(0, 8, unroll=2)
     def _(f):
         blocks = [normalized(f, mine, 8) for mine in (True, False)]
         cols = [feature_columns(f, mine) for mine in (True, False)]
@@ -581,40 +594,48 @@
         hid[0, side] = (gate / (1.0 + jnp.exp(-gate)) * accu[side]).astype(BF)
     send_hid = remote(hid.at[0], hid.at[1], hd_send, hd_recv, partner)
     send_hid.start()
-    for copy in down_local:
-        copy.wait()
-    for copy in down_remote:
-        copy.wait_recv()
-    for pair in range(2):
-        if pair == 1:
-            send_hid.wait_recv()
-
-        @pl.loop(0, 8)
+    wait_bytes(wd.at[core], dl_sem)
+    wait_bytes(wd.at[1 - core], dr_sem)
+    send_hid.wait_recv()
+
+    def project_down(wave):
+        rows = pl.ds(128 * wave, 128)
+
+        @pl.loop(0, 8, unroll=2)
         def _(f):
-            product = dot_nn(hid[pair, 0], wd[0, f]) + dot_nn(hid[pair, 1], wd[1, f])
-            spread(pair, f, product)
-
-        units(scatter_first, 2 * pair, 2 * pair + 2)
+            left = [jnp.concatenate([hid[0, side, rows], hid[1, side, rows]], axis=0) for side in range(2)]
+            spread(wave, f, dot_nn(left[0], wd[0, f]) + dot_nn(left[1], wd[1, f]))
+
+    def finish_second(v):
+        out_ref[token_unit(v), :] = (resid[token_unit(v), :].astype(F32) + final_sum(v)).astype(BF)
+
+    project_down(0)
+    units(scatter_far, wave_a)
+    units(scatter_near, wave_a)
+    project_down(1)
+    units(scatter_far, wave_b)
+    units(s1, wave_a)
+    units(scatter_near, wave_b)
     gather_drain()
-
-    def finish_second(v, total):
-        out_ref[token_unit(v), :] = (resid[token_unit(v), :].astype(F32) + total).astype(BF)
-
-    scatter_rest(finish_second)
+    units(s1, wave_b)
+    for k in (3, 2, 1):
+        units(s2(k))
+    units(s3)
+    units(finish_second)
     scatter_drain()
-    for d in range(1, 16):
-        stat_copy(0, d).wait_send()
-        stat_copy(1, d).wait_send()
-    for e in range(1, 8):
-        root_copy(0, e).wait_send()
-        root_copy(1, e).wait_send()
-    for d in range(1, 8):
-        kv_copy(d).wait_send()
+
+    wait_bytes(stats.at[pl.ds(1, 15)], st_send)
+    wait_bytes(sums.at[pl.ds(1, 15)], su_send)
+    for phase in range(2):
+        wait_bytes(roots.at[phase, pl.ds(1, 7)], ro_send.at[phase])
+    wait_bytes(kvall.at[core, pl.ds(0, 7)], kv_send)
     forward.wait_send()
     send_att.wait_send()
     send_hid.wait_send()
-    for copy in remote_copies + out_remote + down_remote:
+    for copy in remote_copies:
         copy.wait_send()
+    wait_bytes(wo.at[core], os_sem)
+    wait_bytes(wd.at[core], ds_sem)
 
 
 def rotary_tables():
@@ -678,12 +699,11 @@
             dma((4,)), dma((4, 12)),
             dma((2,)), dma((2,)),
             dma((4,)), dma((4, 10)),
-            dma((16,)), dma((16,)), dma((16,)), dma((16,)), dma((2, 8)), dma((2, 8)),
-            dma((8,)), dma((8,)),
+            dma, dma, dma, dma, dma((2,)), dma((2,)),
+            dma, dma,
             dma, dma, dma, dma, dma, dma,
             dma((9,)), dma((5,)), dma((5,)),
-            dma((8,)), dma((8,)), dma((8,)),
-            dma((8,)), dma((8,)), dma((8,)),
+            dma, dma, dma, dma, dma, dma,
         ],
         compiler_params=pltpu.CompilerParams(
             collective_id=0, has_side_effects=True, vmem_limit_bytes=60 * 1024 * 1024

time: 131 us -> 136 us (1.038)
  Pallas kernels: 129 us -> 135 us
    pallas_call x1, Pallas kernels: 129 us -> 135 us  [shards(): pl.pallas_call(kernel, out_shape=jax.ShapeDtypeStruct((64, BLOCK), BF), i...]
where the time goes in v5:
time: 136 us
  Pallas kernels  135 us (99%)
  local copies, waits for them, and re-layouts  1.47 us (1%)
    pallas_call x1, Pallas kernels, shards(): pl.pallas_call(kernel, out_shape=jax.ShapeDtypeStruct((64, BLOCK), BF), i...  135 us

profile of v5, /device:TPU:0, one launch (start us, length us, event | category | flops | bytes accessed | tf_op | source)
XLA Modules:
  0.0 136.2 jit_solution(15075036106085727382)
XLA Ops:
  0.0 134.7 %layer.1 = bf16[64,512]{1,0:T(8,128)(2,1)} custom-call(bf16[64,512]{1,0:T(8,128)(2,1)} %tok_ref.1, s32[32]{0:T(128)} %segment_ref.1, bf16[512]{0:T(512)(128)(2,1)} %gain_ref.1, bf16[512]{0:T(512)(128)(2,1)} %ffn_gain_ref.1, bf16[1024]{0:T(1024)(128)(2,1)} %query_bias_ref.1, bf16[128]{0:T(256)(128)(2,1)} %value_bias_ref.1, bf16[64,8192]{1,0:T(8,128)(2,1)} %wq_hbm.1, ...), custom_call_target="tpu_custom_call" | custom-call | tf_op jit(solution)/shard_map/layer/pallas_call | solution.py:663
  134.7 1.5 %copy.19 = bf16[64,512]{1,0:T(8,128)(2,1)} copy(bf16[64,512]{1,0:T(8,128)(2,1)} %layer.1) | data formatting | bytes 131072

commit v6 on v5

--- a/solution.py
+++ b/solution.py
@@ -84,8 +84,8 @@
     def device(x, y, z):
         return (lax.rem(y, 2) * 4 + x, lax.div(y, 2) * 8 + z * 2 + core)
 
-    own_orders = [(0, 1), (2 * core, 1), (1 + core, 0), (1, core)]
-    other_orders = [(2 - core, 0), (1, 1 - core)]
+    own_orders = [(lax.rem(bulk + 2, 3), 0) for bulk in (core, 2 * core, 1 - core, 2 - core)]
+    other_orders = [(lax.rem(bulk + 2, 3), 0) for bulk in (core, 1 + core)]
 
     def neighbour(v, level, sign):
         bulk, choice = own_orders[v]
@@ -220,7 +220,7 @@
             ag.at[2 + j, pl.ds(16 * k, 16)], xb.at[j, pl.ds(16 * k, 16)], px_send.at[j], px_recv.at[j], partner
         )
 
-    wave_a, wave_b, in_order = (0, 2), (1, 3), (0, 2, 1, 3)
+    wave_a, wave_b, in_order = (0, 1), (2, 3), (0, 2, 1, 3)
 
     def units(body, which=in_order):
         for v in which:
@@ -270,14 +270,26 @@
             px_copy(v - 2, 1).start()
             px_copy(v - 2, 2).start()
 
+    def passing_k(k):
+        def step(v):
+            gather_arrive(v, 4 + k, 8 + k)
+            gather_start(v, f"pass3_{k}_3", f"pass3_{k}_1")
+            if v >= 2 and k == 3:
+                px_copy(v - 2, 1).start()
+                px_copy(v - 2, 2).start()
+
+        return step
+
     def t5(v):
         gather_arrive(v, 3)
         if v >= 2:
             px_copy(v - 2, 3).start()
 
-    def gather_end():
+    def gather_own():
         for v in (2, 3, 0, 1):
             t5(v)
+
+    def gather_other():
         for j in range(2):
             wait_bytes(xb.at[j], px_recv.at[j])
 
@@ -383,14 +395,10 @@
             pltpu.make_async_copy(blocks, blocks, rs_send.at[v]).wait()
 
     def spread(wave, f, product):
-        for j, v in enumerate((wave, 2 + wave)):
+        for j, v in enumerate((2 * wave, 2 * wave + 1)):
             for i, at in enumerate(places(unit_strides[v], f)):
                 row = 128 * j + 16 * i
                 part[v, at] = product[row : row + 16]
-
-    def wave_rows(ref, wave):
-        rows = pl.ds(128 * wave, 128)
-        return jnp.concatenate([ref[0, rows], ref[1, rows]], axis=0)
 
     for v in range(4):
         ag[v, 0] = tok_ref[token_unit(v), :]
@@ -416,9 +424,10 @@
     units(t2)
     units(t3)
     units(t4)
-    units(passing)
+    for k in (1, 2, 3):
+        units(passing_k(k))
     collect_roots(0)
-    gather_end()
+    gather_own()
     documents = jnp.sum(
         jnp.where(lax.broadcasted_iota(jnp.int32, (16, 16, 128), 1) == 1, stats[...], 0.0), axis=1
     )
@@ -429,9 +438,12 @@
 
     acckv[...] = jnp.zeros_like(acckv)
 
-    @pl.loop(0, 8, unroll=2)
-    def _(f):
-        for mine in (True, False):
+    for mine in (True, False):
+        if not mine:
+            gather_other()
+
+        @pl.loop(0, 8, unroll=4)
+        def _(f):
             cols = feature_columns(f, mine)
             weights = [wkv[side, kind, :, cols].astype(F32) for kind in range(2) for side in range(2)]
             weights = jnp.concatenate(weights, axis=0).astype(BF)
@@ -450,7 +462,7 @@
 
     accq[...] = jnp.zeros_like(accq)
 
-    @pl.loop(0, 8, unroll=2)
+    @pl.loop(0, 8, unroll=4)
     def _(f):
         for mine in (True, False):
             cols = feature_columns(f, mine)
@@ -461,10 +473,6 @@
     own_rows = pl.ds(pl.multiple_of(256 * core, 256), 256)
     turned = jnp.concatenate([query[:, 64:], query[:, :64]], axis=1)
     queries = (query * cosq[own_rows, :] + turned * sinq[own_rows, :]).astype(BF)
-
-    wait_bytes(kvall.at[core, pl.ds(0, 7)], kv_recv)
-    forward = remote(kvall.at[core], kvall.at[core], kf_send, kf_recv, partner)
-    forward.start()
 
     def token_parts(index, own_core):
         item, low, along, row = (
@@ -500,6 +508,9 @@
 
     value_bias = jnp.transpose(jnp.broadcast_to(bias[8:9], (128, 128)))
     value_bias = jnp.concatenate([value_bias] * 2, axis=1)
+    wait_bytes(kvall.at[core, pl.ds(0, 7)], kv_recv)
+    forward = remote(kvall.at[core], kvall.at[core], kf_send, kf_recv, partner)
+    forward.start()
     remote(kvall.at[1 - core], kvall.at[1 - core], kf_send, kf_recv, partner).wait_recv()
     key_parts, value_parts = [], []
     for side in range(2):
@@ -523,13 +534,12 @@
 
     wait_bytes(wo.at[core], ol_sem)
     wait_bytes(wo.at[1 - core], or_sem)
-    send_att.wait_recv()
 
     def project_out(wave):
-        @pl.loop(0, 8, unroll=2)
+        @pl.loop(0, 8, unroll=4)
         def _(f):
             weights = jnp.concatenate([wo[0, f], wo[1, f]], axis=0)
-            spread(wave, f, dot_nn(wave_rows(att, wave), weights))
+            spread(wave, f, dot_nn(att[wave], weights))
 
     def finish_first(v):
         block = (tok_ref[token_unit(v), :].astype(F32) + final_sum(v)).astype(BF)
@@ -539,40 +549,31 @@
 
     project_out(0)
     units(scatter_far, wave_a)
-    units(scatter_near, wave_a)
+    send_att.wait_recv()
     project_out(1)
     units(scatter_far, wave_b)
-    units(s1, wave_a)
-    units(scatter_near, wave_b)
+    units(scatter_near)
     gather_drain()
+    units(s1)
     for k in (3, 2, 1):
-        units(s2(k), wave_a)
-    units(s1, wave_b)
-    units(s3, wave_a)
-    for k in (3, 2, 1):
-        units(s2(k), wave_b)
-    units(finish_first, wave_a)
-    units(s3, wave_b)
-    units(t1, wave_a)
-    units(t2, wave_a)
-    units(finish_first, wave_b)
+        units(s2(k))
+    units(s3)
+    units(finish_first)
     square_sums = square_row(resid[...].astype(F32))
     row = lax.broadcasted_iota(jnp.int32, (8, 128), 0)
     sums[0] = jnp.where(row == 0, square_sums, jnp.zeros((8, 128), F32))
     for d in range(1, 16):
         stat_copy(1, d).start()
-    units(t3, wave_a)
-    units(t4, wave_a)
-    units(t1, wave_b)
-    units(t2, wave_b)
+    units(t1)
+    units(t2)
     spread_roots(1)
-    units(t3, wave_b)
+    units(t3)
     scatter_drain()
-    units(passing, wave_a)
-    units(t4, wave_b)
+    units(t4)
+    for k in (1, 2, 3):
+        units(passing_k(k))
     collect_roots(1)
-    units(passing, wave_b)
-    gather_end()
+    gather_own()
     for copy in local_copies[3:]:
         copy.wait()
     for copy in remote_copies[3:]:
@@ -581,13 +582,17 @@
     accg[...] = jnp.zeros_like(accg)
     accu[...] = jnp.zeros_like(accu)
 
-    @pl.loop(0, 8, unroll=2)
-    def _(f):
-        blocks = [normalized(f, mine, 8) for mine in (True, False)]
-        cols = [feature_columns(f, mine) for mine in (True, False)]
-        for side in range(2):
-            accg[side] += dot_nt(blocks[0], wg[side, :, cols[0]]) + dot_nt(blocks[1], wg[side, :, cols[1]])
-            accu[side] += dot_nt(blocks[0], wu[side, :, cols[0]]) + dot_nt(blocks[1], wu[side, :, cols[1]])
+    for mine in (True, False):
+        if not mine:
+            gather_other()
+
+        @pl.loop(0, 8, unroll=4)
+        def _(f):
+            block = normalized(f, mine, 8)
+            cols = feature_columns(f, mine)
+            for side in range(2):
+                accg[side] += dot_nt(block, wg[side, :, cols])
+                accu[side] += dot_nt(block, wu[side, :, cols])
 
     for side in range(2):
         gate = accg[side]
@@ -596,28 +601,23 @@
     send_hid.start()
     wait_bytes(wd.at[core], dl_sem)
     wait_bytes(wd.at[1 - core], dr_sem)
-    send_hid.wait_recv()
 
     def project_down(wave):
-        rows = pl.ds(128 * wave, 128)
-
-        @pl.loop(0, 8, unroll=2)
+        @pl.loop(0, 8, unroll=4)
         def _(f):
-            left = [jnp.concatenate([hid[0, side, rows], hid[1, side, rows]], axis=0) for side in range(2)]
-            spread(wave, f, dot_nn(left[0], wd[0, f]) + dot_nn(left[1], wd[1, f]))
+            spread(wave, f, dot_nn(hid[wave, 0], wd[0, f]) + dot_nn(hid[wave, 1], wd[1, f]))
 
     def finish_second(v):
         out_ref[token_unit(v), :] = (resid[token_unit(v), :].astype(F32) + final_sum(v)).astype(BF)
 
     project_down(0)
     units(scatter_far, wave_a)
-    units(scatter_near, wave_a)
+    send_hid.wait_recv()
     project_down(1)
     units(scatter_far, wave_b)
-    units(s1, wave_a)
-    units(scatter_near, wave_b)
+    units(scatter_near)
     gather_drain()
-    units(s1, wave_b)
+    units(s1)
     for k in (3, 2, 1):
         units(s2(k))
     units(s3)

time: 136 us -> 123 us (0.904)
  Pallas kernels: 135 us -> 121 us
    pallas_call x1, Pallas kernels: 135 us -> 121 us  [shards(): pl.pallas_call(kernel, out_shape=jax.ShapeDtypeStruct((64, BLOCK), BF), i...]
where the time goes in v6:
time: 123 us
  Pallas kernels  121 us (98%)
  local copies, waits for them, and re-layouts  1.47 us (1%)
    pallas_call x1, Pallas kernels, shards(): pl.pallas_call(kernel, out_shape=jax.ShapeDtypeStruct((64, BLOCK), BF), i...  121 us

profile of v6, /device:TPU:0, one launch (start us, length us, event | category | flops | bytes accessed | tf_op | source)
XLA Modules:
  0.0 122.9 jit_solution(8575735360854579620)
XLA Ops:
  0.0 121.4 %layer.1 = bf16[64,512]{1,0:T(8,128)(2,1)} custom-call(bf16[64,512]{1,0:T(8,128)(2,1)} %tok_ref.1, s32[32]{0:T(128)} %segment_ref.1, bf16[512]{0:T(512)(128)(2,1)} %gain_ref.1, bf16[512]{0:T(512)(128)(2,1)} %ffn_gain_ref.1, bf16[1024]{0:T(1024)(128)(2,1)} %query_bias_ref.1, bf16[128]{0:T(256)(128)(2,1)} %value_bias_ref.1, bf16[64,8192]{1,0:T(8,128)(2,1)} %wq_hbm.1, ...), custom_call_target="tpu_custom_call" | custom-call | tf_op jit(solution)/shard_map/layer/pallas_call | solution.py:663
  121.4 1.5 %copy.19 = bf16[64,512]{1,0:T(8,128)(2,1)} copy(bf16[64,512]{1,0:T(8,128)(2,1)} %layer.1) | data formatting | bytes 131072

commit v7 on v6

--- a/solution.py
+++ b/solution.py
@@ -229,6 +229,8 @@
     def gather_begin(v):
         for sign in (1, 3, 2):
             gather_copy(f"own1_{sign}", v).start()
+
+    def gather_more(v):
         for sign in (1, 3):
             gather_copy(f"one3_0_{sign}", v).start()
         for sign in (1, 3, 2):
@@ -334,29 +336,36 @@
             part[v, pl.ds(src, count)] + rb[v, pl.ds(place_at, count)].astype(F32)
         ).astype(BF)
 
-    def scatter_far(v):
+    def scatter_far(which):
         for k in (3, 1, 2, 0):
-            cast(v, 48 + 4 * k)
-            rs_start(v, f"far3_{k}")
-
-    def scatter_near(v):
-        for k in (3, 2):
-            cast(v, 32 + 4 * k)
-            rs_start(v, f"down3_{k}")
-        cast(v, 16 + 4 * 1)
-        rs_start(v, "up3_1")
-
-    def s1(v):
-        for k in (3, 2):
-            rs_arrive(v, k)
-            cast_sum(v, 16 + 4 * k, 4 * (3 - k))
-            rs_start(v, f"up3_{k}")
-        for k in (1, 0):
-            rs_arrive(v, k)
-            cast_sum(v, 32 + 4 * k, 8 + 4 * (1 - k))
-            rs_start(v, f"down3_{k}")
-        cast(v, 16)
-        rs_start(v, "up3_0")
+            for v in which:
+                cast(v, 48 + 4 * k)
+                rs_start(v, f"far3_{k}")
+
+    def scatter_near():
+        for v in in_order:
+            cast(v, 32 + 4 * 3)
+            rs_start(v, "down3_3")
+        for v in in_order:
+            cast(v, 16 + 4 * 1)
+            rs_start(v, "up3_1")
+        for v in in_order:
+            cast(v, 32 + 4 * 2)
+            rs_start(v, "down3_2")
+
+    def scatter_relay():
+        for k, other in ((3, 1), (2, 0)):
+            for v in in_order:
+                rs_arrive(v, k)
+                cast_sum(v, 16 + 4 * k, 4 * (3 - k))
+                rs_start(v, f"up3_{k}")
+            for v in in_order:
+                rs_arrive(v, other)
+                cast_sum(v, 32 + 4 * other, 8 + 4 * (1 - other))
+                rs_start(v, f"down3_{other}")
+        for v in in_order:
+            cast(v, 16)
+            rs_start(v, "up3_0")
 
     def total3(v, k):
         rs_arrive(v, 4 + k)
@@ -412,6 +421,7 @@
     bias[8:9] = value_bias_ref[...].astype(F32).reshape(1, 128)
     pl.semaphore_wait(barrier, len(greeted))
     units(gather_begin)
+    units(gather_more)
     for d in range(1, 16):
         stat_copy(0, d).start()
     for copy in remote_copies[:3]:
@@ -422,8 +432,8 @@
     for copy in out_remote + remote_copies[3:] + down_remote:
         copy.start()
     units(t2)
+    units(t4)
     units(t3)
-    units(t4)
     for k in (1, 2, 3):
         units(passing_k(k))
     collect_roots(0)
@@ -548,17 +558,18 @@
         gather_begin(v)
 
     project_out(0)
-    units(scatter_far, wave_a)
+    scatter_far(wave_a)
     send_att.wait_recv()
     project_out(1)
-    units(scatter_far, wave_b)
-    units(scatter_near)
+    scatter_far(wave_b)
+    scatter_near()
     gather_drain()
-    units(s1)
+    scatter_relay()
     for k in (3, 2, 1):
         units(s2(k))
     units(s3)
     units(finish_first)
+    units(gather_more)
     square_sums = square_row(resid[...].astype(F32))
     row = lax.broadcasted_iota(jnp.int32, (8, 128), 0)
     sums[0] = jnp.where(row == 0, square_sums, jnp.zeros((8, 128), F32))
@@ -567,9 +578,9 @@
     units(t1)
     units(t2)
     spread_roots(1)
+    units(t4)
     units(t3)
     scatter_drain()
-    units(t4)
     for k in (1, 2, 3):
         units(passing_k(k))
     collect_roots(1)
@@ -611,13 +622,13 @@
         out_ref[token_unit(v), :] = (resid[token_unit(v), :].astype(F32) + final_sum(v)).astype(BF)
 
     project_down(0)
-    units(scatter_far, wave_a)
+    scatter_far(wave_a)
     send_hid.wait_recv()
     project_down(1)
-    units(scatter_far, wave_b)
-    units(scatter_near)
+    scatter_far(wave_b)
+    scatter_near()
     gather_drain()
-    units(s1)
+    scatter_relay()
     for k in (3, 2, 1):
         units(s2(k))
     units(s3)

time: 123 us -> 121 us (0.984)
  Pallas kernels: 121 us -> 119 us
    pallas_call x1, Pallas kernels: 121 us -> 119 us  [shards(): pl.pallas_call(kernel, out_shape=jax.ShapeDtypeStruct((64, BLOCK), BF), i...]
where the time goes in v7:
time: 121 us
  Pallas kernels  119 us (98%)
  local copies, waits for them, and re-layouts  1.47 us (1%)
    pallas_call x1, Pallas kernels, shards(): pl.pallas_call(kernel, out_shape=jax.ShapeDtypeStruct((64, BLOCK), BF), i...  119 us

profile of v7, /device:TPU:0, one launch (start us, length us, event | category | flops | bytes accessed | tf_op | source)
XLA Modules:
  0.0 120.8 jit_solution(1873766023176274534)
XLA Ops:
  0.0 119.3 %layer.1 = bf16[64,512]{1,0:T(8,128)(2,1)} custom-call(bf16[64,512]{1,0:T(8,128)(2,1)} %tok_ref.1, s32[32]{0:T(128)} %segment_ref.1, bf16[512]{0:T(512)(128)(2,1)} %gain_ref.1, bf16[512]{0:T(512)(128)(2,1)} %ffn_gain_ref.1, bf16[1024]{0:T(1024)(128)(2,1)} %query_bias_ref.1, bf16[128]{0:T(256)(128)(2,1)} %value_bias_ref.1, bf16[64,8192]{1,0:T(8,128)(2,1)} %wq_hbm.1, ...), custom_call_target="tpu_custom_call" | custom-call | tf_op jit(solution)/shard_map/layer/pallas_call | solution.py:674
  119.3 1.5 %copy.19 = bf16[64,512]{1,0:T(8,128)(2,1)} copy(bf16[64,512]{1,0:T(8,128)(2,1)} %layer.1) | data formatting | bytes 131072

commit v8 on v7

--- a/solution.py
+++ b/solution.py
@@ -565,8 +565,7 @@
     scatter_near()
     gather_drain()
     scatter_relay()
-    for k in (3, 2, 1):
-        units(s2(k))
+    units(lambda v: [s2(k)(v) for k in (3, 2, 1)])
     units(s3)
     units(finish_first)
     units(gather_more)
@@ -629,8 +628,7 @@
     scatter_near()
     gather_drain()
     scatter_relay()
-    for k in (3, 2, 1):
-        units(s2(k))
+    units(lambda v: [s2(k)(v) for k in (3, 2, 1)])
     units(s3)
     units(finish_second)
     scatter_drain()

time: 121 us -> 121 us (level)
  no operation moved by 1% of the time
where the time goes in v8:
time: 121 us
  Pallas kernels  119 us (98%)
  local copies, waits for them, and re-layouts  1.47 us (1%)
    pallas_call x1, Pallas kernels, shards(): pl.pallas_call(kernel, out_shape=jax.ShapeDtypeStruct((64, BLOCK), BF), i...  119 us

profile of v8, /device:TPU:0, one launch (start us, length us, event | category | flops | bytes accessed | tf_op | source)
XLA Modules:
  0.0 120.7 jit_solution(9183094231480699018)
XLA Ops:
  0.0 119.3 %layer.1 = bf16[64,512]{1,0:T(8,128)(2,1)} custom-call(bf16[64,512]{1,0:T(8,128)(2,1)} %tok_ref.1, s32[32]{0:T(128)} %segment_ref.1, bf16[512]{0:T(512)(128)(2,1)} %gain_ref.1, bf16[512]{0:T(512)(128)(2,1)} %ffn_gain_ref.1, bf16[1024]{0:T(1024)(128)(2,1)} %query_bias_ref.1, bf16[128]{0:T(256)(128)(2,1)} %value_bias_ref.1, bf16[64,8192]{1,0:T(8,128)(2,1)} %wq_hbm.1, ...), custom_call_target="tpu_custom_call" | custom-call | tf_op jit(solution)/shard_map/layer/pallas_call | solution.py:672
  119.3 1.5 %copy.19 = bf16[64,512]{1,0:T(8,128)(2,1)} copy(bf16[64,512]{1,0:T(8,128)(2,1)} %layer.1) | data formatting | bytes 131072
